TPU v7x, 256 devices: a whole 4x4x8 slice. The times are simulated.
256 devices in a mesh: ingest: 128 (over x, z, y), span: 2 (over core).
Axes of the slice: x: 4, y: 4, z: 8, core: 2. Of those that a mesh axis runs over, the one named last changes fastest.
Arguments:
- embeddings: bfloat16 [131072, 768], P(('ingest', 'span')), may hold values from -100 to 100
- cluster_id: int32 [131072], P(('ingest', 'span')), may hold values from 0 to 127, as said below
- rank: int32 [131072], P(('ingest', 'span')), may hold values from 0 to 131071, each once
Outputs:
- max_cosine: float32 [131072], P(('ingest', 'span'))
Inputs may be any that keep to these rules, and one draw needn't show every extreme that they name: `cluster_id`: the 512 embeddings of each device name one cluster at most 8 times, and some cluster exactly 8 times. `rank`: every value once.
All inputs are finite; a program needn't handle non-finite values.
Results may differ from a plain program's by a relative error of at most 0.00054.
Values may be sent and summed in bfloat16 or wider, within the bound.
A program may use at most 64 MiB of HBM per device.

v0:
```python
import jax
import jax.numpy as jnp
from jax import lax
from jax.sharding import PartitionSpec as P

beyond_rank = 2**30


def normalize(embeddings):
    widened = embeddings.astype(jnp.float32)
    return (widened * lax.rsqrt(jnp.sum(widened * widened, axis=1, keepdims=True) + 1e-06)).astype(
        jnp.bfloat16
    )


def tile_maxima(queries, query_rank, candidates, candidate_rank):
    scores = jnp.einsum("qd,kd->qk", queries, candidates, preferred_element_type=jnp.float32)
    earlier = candidate_rank[None, :] < query_rank[:, None]
    return jnp.max(jnp.where(earlier, scores, -1.0), axis=1)


def blocked_rows(queries, query_rank, candidates, candidate_rank):
    total = queries.shape[0]
    height = min(512, total)
    grouped = queries.reshape(total // height, height, queries.shape[1])
    rank_groups = query_rank.reshape(total // height, height)
    maxima = lax.map(
        lambda grouping: tile_maxima(grouping[0], grouping[1], candidates, candidate_rank),
        (grouped, rank_groups),
    )
    return maxima.reshape(total)


def body(embeddings, cluster_id, rank):
    nodes = lax.axis_size("ingest")
    rows = embeddings.shape[0]
    width = embeddings.shape[1]
    capacity = 2 * rows // nodes
    slots = nodes * capacity
    normed = normalize(embeddings)
    owner_table = (cluster_id[:, None] == jnp.arange(nodes, dtype=jnp.int32)[None, :]).astype(
        jnp.int32
    )
    before = jnp.cumsum(owner_table, axis=0) - owner_table
    position = jnp.sum(before * owner_table, axis=1)
    target = cluster_id * capacity + position
    outgoing = (
        jnp.zeros((slots, width), jnp.bfloat16)
        .at[target]
        .set(normed)
        .reshape(nodes, capacity, width)
    )
    outgoing_rank = (
        jnp.full((slots,), beyond_rank, jnp.int32).at[target].set(rank).reshape(nodes, capacity)
    )
    arrived, arrived_rank = (
        lax.all_to_all(outgoing, "ingest", split_axis=0, concat_axis=0, tiled=True),
        lax.all_to_all(outgoing_rank, "ingest", split_axis=0, concat_axis=0, tiled=True),
    )
    arrived = arrived.reshape(slots, width)
    arrived_rank = arrived_rank.reshape(slots)
    highest = jnp.maximum(
        jnp.full((slots,), -1.0, jnp.float32),
        blocked_rows(
            arrived,
            arrived_rank,
            lax.all_gather(arrived, "span", axis=0, tiled=True),
            lax.all_gather(arrived_rank, "span", axis=0, tiled=True),
        ),
    )
    returned = lax.all_to_all(
        highest.reshape(nodes, capacity), "ingest", split_axis=0, concat_axis=0, tiled=True
    )
    return returned.reshape(slots)[target]


def solution(mesh):
    in_specs = (P(("ingest", "span"), None), P(("ingest", "span")), P(("ingest", "span")))
    out_specs = P(("ingest", "span"))
    return jax.shard_map(body, mesh=mesh, in_specs=in_specs, out_specs=out_specs, check_vma=False)
```

profile of v0, /device:TPU:1, one launch (start us, length us, event | category | flops | bytes accessed | tf_op | source)
XLA Modules:
  0.0 132.6 jit_solution(8449085722662017891)
XLA Ops:
  6.5 0.0 copy-start.2
  6.5 0.0 copy-start.1
  6.5 0.0 all-gather.2.cloned.1.call-start
  6.5 0.9 copy.6
  7.4 0.2 fusion.11
  7.7 0.9 fusion.10
  8.6 0.0 copy-done.2
  8.7 0.0 copy-done.1
  8.7 0.2 fusion.3
  8.9 3.1 %scatter_custom_fusion.1 = bf16[1024,768]{1,0:T(8,128)(2,1)S(1)} fusion(s32[512]{0:T(512)S(1)} %compare_select_fusion, bf16[512,768]{1,0:T(8,128)(2,1)S(1)} %copy-done.1, f32[512]{0:T(512)S(1)} %add_rsqrt_fusion, bf16[]{:T(256)} %constant.9.clone.1), kind=kCustom, calls=%fused_computation.12 | custom fusion | flops 1179648 | bytes 2361346 | tf_op jit(solution)/shard_map/scatter | solution.py:50
  12.0 55.0 %all_to_all.20 = bf16[128,8,768]{2,1,0:T(8,128)(2,1)} all-to-all(bf16[128,8,768]{2,1,0:T(8,128)(2,1)S(1)} %bitcast.36), channel_id=1, replica_groups=mesh['ingest'=128,'span'=2] {'ingest'}, dimensions={0} | all-to-all | bytes 3145728 | tf_op jit(solution)/shard_map/all_to_all | solution.py:57
  67.0 0.0 copy-start
  67.0 0.0 all-gather.2.cloned.1.call-update
  67.0 2.7 %scatter_custom_fusion = s32[1024]{0:T(1024)S(1)} fusion(s32[512]{0:T(512)S(1)} %compare_select_fusion, s32[512]{0:T(512)} %param.7, s32[]{:T(128)} %constant.24.clone.1), kind=kCustom, calls=%fused_computation.29 | custom fusion | bytes 4608 | tf_op jit(solution)/shard_map/scatter | solution.py:54
  69.8 0.7 all_to_all.13
  70.5 8.9 %all-to-all-start = ((s32[128,1,8]{2,1,0:T(1,128)}), s32[128,1,8]{2,1,0:T(1,128)S(1)}, u32[]{:S(2)}, u32[]{:S(2)}) async-start(s32[128,1,8]{2,1,0:T(1,128)} %bitcast.7), calls=%async_computation | async-start | bytes 131072 | tf_op jit(solution)/shard_map/all_to_all | solution.py:58
  79.4 10.5 %all-to-all-done = s32[128,1,8]{2,1,0:T(1,128)S(1)} async-done(((s32[128,1,8]{2,1,0:T(1,128)}), s32[128,1,8]{2,1,0:T(1,128)S(1)}, u32[]{:S(2)}, u32[]{:S(2)}) %all-to-all-start) | async-done | bytes 4128 | tf_op jit(solution)/shard_map/all_to_all | solution.py:58
  90.0 0.5 broadcast.57
  90.5 0.7 reduce.8
  91.2 0.1 reshape.62
  91.3 0.1 reshape_reshape.6
  91.4 4.3 %all_gather.6 = s32[2048]{0:T(1024)S(1)} all-gather(s32[1024]{0:T(1024)S(1)} %reshape.62), channel_id=1, replica_groups=mesh['ingest'=128,'span'=2] {'span'}, dimensions={0}, use_global_device_ids=true | all-gather | bytes 12288 | tf_op jit(solution)/shard_map/all_gather | solution.py:68
  95.7 0.0 all-gather.2.cloned.1.call-done
  95.7 0.0 copy-done
  95.7 7.8 %while.10 = (s32[]{:T(128)}, f32[2,512]{1,0:T(2,128)S(1)}, s32[2048]{0:T(1024)S(1)}, s32[2,512]{1,0:T(2,128)S(1)}, bf16[2,512,768]{2,1,0:T(8,128)(2,1)S(1)}, /*i...) while((s32[]{:T(128)}, f32[2,512]{1,0:T(2,128)S(1)}, s32[2048]{0:T(1024)S(1)}, s32[2,512]{1,0:T(2,128)S(1)}, ...), condition=%wide.region_8.9_spmd, body=%wide.region_6.8_spmd.sunk | while | flops 1613757952 | bytes 3952745 | solution.py:27
  95.7 3.8 %select_reduce_fusion.2 = f32[512]{0:T(512)S(1)} fusion(bf16[2048,768]{1,0:T(8,128)(2,1)} %get-tuple-element.108, s32[2048]{0:T(1024)S(1)} %get-tuple-element.105, s32[512]{0:T(512)S(1)} %bitcast.41, bf16[2,512,768]{2,1,0:T(8,128)(2,1)S(1)} %get-tuple-element.107, s32[]{:T(128)S(6)} %copy.13), kind=kOutput, calls=%fused_computation.3.clone.1 | convolution fusion | flops 1613757952 | bytes 3944452 | tf_op jit(solution)/shard_map/while/body/eval_jaxpr/qd,kd->qk/dot_general | solution.py:17
  99.6 3.8 %select_reduce_fusion.2 = f32[512]{0:T(512)S(1)} fusion(bf16[2048,768]{1,0:T(8,128)(2,1)} %get-tuple-element.108, s32[2048]{0:T(1024)S(1)} %get-tuple-element.105, s32[512]{0:T(512)S(1)} %bitcast.41, bf16[2,512,768]{2,1,0:T(8,128)(2,1)S(1)} %get-tuple-element.107, s32[]{:T(128)S(6)} %copy.13), kind=kOutput, calls=%fused_computation.3.clone.1 | convolution fusion | flops 1613757952 | bytes 3944452 | tf_op jit(solution)/shard_map/while/body/eval_jaxpr/qd,kd->qk/dot_general | solution.py:17
  103.5 0.7 max_broadcast_in_dim.15
  104.2 6.2 %all-to-all-start.2 = ((f32[128,1,8]{2,1,0:T(1,128)}), f32[128,1,8]{2,1,0:T(1,128)S(1)}, u32[]{:S(2)}, u32[]{:S(2)}) async-start(f32[128,1,8]{2,1,0:T(1,128)} %bitcast.11), calls=%async_computation.2 | async-start | bytes 131072 | tf_op jit(solution)/shard_map/all_to_all | solution.py:71
  110.4 10.6 %all-to-all-done.2 = f32[128,1,8]{2,1,0:T(1,128)S(1)} async-done(((f32[128,1,8]{2,1,0:T(1,128)}), f32[128,1,8]{2,1,0:T(1,128)S(1)}, u32[]{:S(2)}, u32[]{:S(2)}) %all-to-all-start.2) | async-done | bytes 4128 | tf_op jit(solution)/shard_map/all_to_all | solution.py:71
  120.9 0.5 broadcast.58
  121.4 0.8 reduce.9
  122.2 0.1 reshape.65
  122.3 3.4 %gather_fusion = f32[512]{0:T(512)} fusion(f32[1024]{0:T(1024)S(1)} %reshape.65, s32[1024]{0:T(1024)S(1)} %pad_clamp_fusion), kind=kCustom, calls=%fused_computation | custom fusion | bytes 6144 | tf_op jit(solution)/shard_map/gather | solution.py:74
  (15 shorter events, 0.2 us)
Async XLA Ops:
  6.5 2.1 %copy-start.2 = (s32[512]{0:T(512)S(1)}, s32[512]{0:T(512)}, u32[]{:S(2)}) copy-start(s32[512]{0:T(512)} %param.6) | copy-start | bytes 6148
  6.5 2.1 %copy-start.1 = (bf16[512,768]{1,0:T(8,128)(2,1)S(1)}, bf16[512,768]{1,0:T(8,128)(2,1)}, u32[]{:S(2)}) copy-start(bf16[512,768]{1,0:T(8,128)(2,1)} %param.5) | copy-start | bytes 2359300
  6.5 89.1 %all-gather.2.cloned.1.call-start = ((), (), s32[]{:S(2)}) async-start(), calls=%async_computation.3 | async-start | bytes 4718592 | tf_op jit(solution)/shard_map/all_gather | solution.py:67
  67.0 28.7 %copy-start = (bf16[128,8,768]{2,1,0:T(8,128)(2,1)S(1)}, bf16[128,8,768]{2,1,0:T(8,128)(2,1)}, u32[]{:S(2)}) copy-start(bf16[128,8,768]{2,1,0:T(8,128)(2,1)} %all_to_all.20) | copy-start | bytes 4718596
  70.5 19.5 %all-to-all-start = ((s32[128,1,8]{2,1,0:T(1,128)}), s32[128,1,8]{2,1,0:T(1,128)S(1)}, u32[]{:S(2)}, u32[]{:S(2)}) async-start(s32[128,1,8]{2,1,0:T(1,128)} %bitcast.7), calls=%async_computation | async-start | bytes 131072 | tf_op jit(solution)/shard_map/all_to_all | solution.py:58
  104.2 16.8 %all-to-all-start.2 = ((f32[128,1,8]{2,1,0:T(1,128)}), f32[128,1,8]{2,1,0:T(1,128)S(1)}, u32[]{:S(2)}, u32[]{:S(2)}) async-start(f32[128,1,8]{2,1,0:T(1,128)} %bitcast.11), calls=%async_computation.2 | async-start | bytes 131072 | tf_op jit(solution)/shard_map/all_to_all | solution.py:71
Sparse Core Ops, SparseCore 0:
  67.2 15.2 all-gather.1
where the time goes:
time: 133 us
  blocking collectives  59.3 us (45%)
  waiting for transfers between devices  21.1 us (16%)
  starting transfers between devices  15.1 us (11%)
  between operations  13.5 us (10%)
  local copies, waits for them, and re-layouts  9.83 us (7%)
  matrix products  7.64 us (6%)
  other arithmetic  6.04 us (5%)
    all_to_all x1, blocking collectives, body(): lax.all_to_all(outgoing, 'ingest', split_axis=0, concat_axis=0, tiled=True)  55 us
    all_to_all x1, waiting for transfers between devices, body(): lax.all_to_all(highest.reshape(nodes, capacity), 'ingest', split_axis=0,...  10.6 us
    all_to_all x1, waiting for transfers between devices, body(): lax.all_to_all(outgoing_rank, 'ingest', split_axis=0, concat_axis=0, tile...  10.5 us
    all_to_all x1, starting transfers between devices, body(): lax.all_to_all(outgoing_rank, 'ingest', split_axis=0, concat_axis=0, tile...  8.93 us
    dot_general x2, matrix products, tile_maxima(): jnp.einsum('qd,kd->qk', queries, candidates, preferred_element_type=jnp.f...  7.64 us
    all_to_all x1, starting transfers between devices, body(): lax.all_to_all(highest.reshape(nodes, capacity), 'ingest', split_axis=0,...  6.17 us
    all_gather x1, blocking collectives, body(): lax.all_gather(arrived_rank, 'span', axis=0, tiled=True)  4.31 us
    gather x1, local copies, waits for them, and re-layouts, body(): return returned.reshape(slots)[target]  3.42 us
  transfers between devices with their start and end apart: 3, of which 2 were waited for; matrix products, arithmetic and copies ran while one was open for 3% of the time, Pallas kernels for 0%

commit v1 on v0

v1 whole, which is shorter than its diff:
```python
import jax
import jax.numpy as jnp
from jax import lax
from jax.experimental import pallas as pl
from jax.experimental.pallas import tpu as pltpu
from jax.sharding import PartitionSpec as P

XS, ZS, YS = 4, 8, 4
PLANE = XS * YS
CAP = 8
BLOCK = PLANE * CAP
BEYOND = float(2**30)
MESH = pl.DeviceIdType.MESH
Z_OFFSETS = (0, 1, 7, 2, 6, 3, 5, 4)
f32, bf16, i32 = jnp.float32, jnp.bfloat16, jnp.int32


def contract_last(a, b):
    return lax.dot_general(a, b, (((1,), (1,)), ((), ())), preferred_element_type=f32)


def kernel(
    emb_hbm, cid_ref, rank_ref, out_ref,
    emb, normed, onehot, snd, zrcv, prcv, own, sib,
    rsnd, zrk, prk, rown, rsib, qrank, acc, res, pres, zres,
    emb_sem, z_send, z_recv, zr_send, zr_recv, p_send, p_recv, pr_send, pr_recv,
    loc, s_send, s_recv, sr_send, sr_recv, o1_send, o1_recv, o2_send, o2_recv, loc_small,
):
    rows = cid_ref.shape[1]
    width = emb.shape[1]
    half = width // 2
    me = lax.axis_index("ingest")
    core = lax.axis_index("span")
    x, z, y = me // (ZS * YS), (me // YS) % ZS, me % YS
    mine = x * YS + y

    def chip(px, pz, py):
        return (px * ZS + pz) * YS + py

    def z_peer(offset):
        return (chip(x, lax.rem(z + offset, ZS), y), core)

    def plane_peer(r):
        px, py = lax.rem(x + r // YS, XS), lax.rem(y + lax.rem(r, YS), YS)
        return px * YS + py, (chip(px, z, py), core)

    sibling = (me, 1 - core)

    load = pltpu.make_async_copy(emb_hbm, emb, emb_sem)
    load.start()
    barrier = pltpu.get_barrier_semaphore()
    for offset in range(1, ZS):
        pl.semaphore_signal(barrier, inc=1, device_id=z_peer(offset), device_id_type=MESH)

    def greet(r, carry):
        pl.semaphore_signal(barrier, inc=1, device_id=plane_peer(r)[1], device_id_type=MESH)
        return carry

    lax.fori_loop(1, PLANE, greet, 0)
    pl.semaphore_signal(barrier, inc=1, device_id=sibling, device_id_type=MESH)

    cid = cid_ref[...]
    cx, cz, cy = cid >> 5, (cid >> 2) & 7, cid & 3
    dz = (cz - z) & 7
    step_of = jnp.where(dz <= 4, 2 * dz - 1, 2 * (ZS - dz))
    step_of = jnp.where(dz == 0, 0, step_of)
    owner = step_of * PLANE + cx * YS + cy
    hot = lax.broadcasted_iota(i32, (ZS * PLANE, rows), 0) == owner
    hot_f = jnp.where(hot, 1.0, 0.0)
    onehot[...] = hot_f.astype(bf16)
    upper = lax.broadcasted_iota(i32, (rows, rows), 0) < lax.broadcasted_iota(i32, (rows, rows), 1)
    before = jnp.dot(onehot[...], jnp.where(upper, 1.0, 0.0).astype(bf16), preferred_element_type=f32)
    place = jnp.sum(hot_f * before, axis=0, keepdims=True).astype(i32)
    slot = owner * CAP + place
    lane = mine * CAP + place
    at_lane = lax.broadcasted_iota(i32, (128, rows), 0) == lane

    number = rank_ref[...] + 1
    table = jnp.zeros((ZS * PLANE, 128), f32)
    for shift in (0, 6, 12):
        digit = ((number >> shift) & 63).astype(f32)
        spread = jnp.where(at_lane, digit, 0.0).astype(bf16)
        table += contract_last(onehot[...], spread) * float(1 << shift)
    for t in range(ZS * PLANE):
        row = table[t : t + 1, :]
        if t < PLANE:
            zrk[0, t] = row
        else:
            rsnd[t // PLANE, t % PLANE] = row

    load.wait()
    wide = emb[...].astype(f32)
    scale = lax.rsqrt(jnp.sum(wide * wide, axis=1, keepdims=True) + 1e-06)
    normed[...] = (wide * scale).astype(bf16)

    def place_rows(first, count):
        span = count * BLOCK
        ids = lax.broadcasted_iota(i32, (span, rows), 0) + first * BLOCK
        pick = jnp.where(ids == slot, 1.0, 0.0).astype(bf16)
        placed = jnp.dot(pick, normed[...], preferred_element_type=f32)
        placed = placed.reshape(count * PLANE, CAP, width)
        paired = jnp.concatenate([placed[:, :, :half], placed[:, :, half:]], axis=1)
        snd[first : first + count] = paired.astype(bf16).reshape(count, PLANE, 2 * CAP, half)

    def send_z(j):
        pltpu.make_async_remote_copy(
            src_ref=snd.at[j], dst_ref=zrcv.at[j], send_sem=z_send, recv_sem=z_recv.at[j],
            device_id=z_peer(Z_OFFSETS[j]), device_id_type=MESH,
        ).start()

    def send_plane(source, j):
        def one(r, carry):
            q, device = plane_peer(r)
            pltpu.make_async_remote_copy(
                src_ref=source.at[j, q], dst_ref=prcv.at[j, mine], send_sem=p_send,
                recv_sem=p_recv.at[j], device_id=device, device_id_type=MESH,
            ).start()
            return carry

        lax.fori_loop(1, PLANE, one, 0)
        pltpu.make_async_copy(source.at[j, mine], prcv.at[j, mine], loc.at[j]).start()

    place_rows(1, 2)
    pl.semaphore_wait(barrier, ZS - 1 + PLANE - 1 + 1)
    for j in range(1, ZS):
        pltpu.make_async_remote_copy(
            src_ref=rsnd.at[j], dst_ref=zrk.at[j], send_sem=zr_send, recv_sem=zr_recv,
            device_id=z_peer(Z_OFFSETS[j]), device_id_type=MESH,
        ).start()
    send_z(1)
    send_z(2)
    place_rows(3, 2)
    send_z(3)
    send_z(4)
    place_rows(5, 2)
    send_z(5)
    send_z(6)
    place_rows(7, 1)
    send_z(7)
    place_rows(0, 1)
    send_plane(snd, 0)

    pltpu.make_async_copy(rsnd.at[pl.ds(1, ZS - 1)], zrk.at[pl.ds(1, ZS - 1)], zr_recv).wait()

    def rank_on(r, carry):
        q, device = plane_peer(r)
        pltpu.make_async_remote_copy(
            src_ref=zrk.at[:, q], dst_ref=prk.at[mine], send_sem=pr_send, recv_sem=pr_recv,
            device_id=device, device_id_type=MESH,
        ).start()
        return carry

    lax.fori_loop(1, PLANE, rank_on, 0)
    own_rank = pltpu.make_async_copy(zrk.at[:, mine], prk.at[mine], loc_small)
    own_rank.start()
    acc[...] = jnp.full(acc.shape, -1.0, f32)
    own_rank.wait()
    pltpu.make_async_copy(prk.at[pl.ds(0, PLANE - 1)], prk.at[pl.ds(0, PLANE - 1)], pr_recv).wait()
    found = jnp.sum(prk[...], axis=0)
    rown[...] = jnp.where(found == 0.0, BEYOND, found - 1.0)
    pltpu.make_async_remote_copy(
        src_ref=rown, dst_ref=rsib, send_sem=sr_send, recv_sem=sr_recv,
        device_id=sibling, device_id_type=MESH,
    ).start()
    for i in range(ZS):
        qrank[i] = jnp.transpose(jnp.broadcast_to(rown[i], (BLOCK, BLOCK)))

    def hand_over(j):
        blocks = prcv.at[j, pl.ds(0, PLANE - 1)]
        pltpu.make_async_copy(blocks, blocks, p_recv.at[j]).wait()
        pltpu.make_async_copy(prcv.at[j, mine], prcv.at[j, mine], loc.at[j]).wait()
        block = prcv[j].astype(f32)
        low = block[:, :CAP, :].reshape(BLOCK, half)
        high = block[:, CAP:, :].reshape(BLOCK, half)
        own[j] = jnp.concatenate([low, high], axis=1).astype(bf16)
        pltpu.make_async_remote_copy(
            src_ref=own.at[j], dst_ref=sib.at[j], send_sem=s_send, recv_sem=s_recv.at[j],
            device_id=sibling, device_id_type=MESH,
        ).start()

    def score(i, j):
        keys = jnp.concatenate([own[j], sib[j]], axis=0)
        scores = contract_last(own[i], keys)
        theirs = qrank[i]
        near = jnp.where(rown[j] < theirs, scores[:, :BLOCK], -1.0)
        far = jnp.where(rsib[j] < theirs, scores[:, BLOCK:], -1.0)
        acc[i] = jnp.maximum(acc[i], jnp.maximum(near, far))

    def scores_of(j):
        pltpu.make_async_copy(sib.at[j], sib.at[j], s_recv.at[j]).wait()
        if j == 0:
            pltpu.make_async_copy(rsib, rsib, sr_recv).wait()
        for i in range(j + 1):
            score(i, j)
        for k in range(j):
            score(j, k)

    hand_over(0)
    for j in range(1, ZS):
        pltpu.make_async_copy(zrcv.at[j], zrcv.at[j], z_recv.at[j]).wait()
        send_plane(zrcv, j)
        if j >= 2:
            hand_over(j - 1)
            scores_of(j - 2)
    scores_of(ZS - 2)
    hand_over(ZS - 1)
    scores_of(ZS - 1)

    for i in range(ZS):
        res[i] = jnp.max(jnp.transpose(acc[i]), axis=0, keepdims=True)

    def give_back(r, carry):
        _, device = plane_peer(r)
        pltpu.make_async_remote_copy(
            src_ref=res, dst_ref=pres.at[mine], send_sem=o1_send, recv_sem=o1_recv,
            device_id=device, device_id_type=MESH,
        ).start()
        return carry

    lax.fori_loop(1, PLANE, give_back, 0)
    own_res = pltpu.make_async_copy(res, pres.at[mine], loc_small)
    own_res.start()
    own_res.wait()
    pltpu.make_async_copy(pres.at[pl.ds(0, PLANE - 1)], pres.at[pl.ds(0, PLANE - 1)], o1_recv).wait()
    for j in range(1, ZS):
        pltpu.make_async_remote_copy(
            src_ref=pres.at[:, j], dst_ref=zres.at[j], send_sem=o2_send, recv_sem=o2_recv,
            device_id=z_peer(ZS - Z_OFFSETS[j]), device_id_type=MESH,
        ).start()
    own_last = pltpu.make_async_copy(pres.at[:, 0], zres.at[0], loc_small)
    own_last.start()
    own_last.wait()
    pltpu.make_async_copy(zres.at[pl.ds(1, ZS - 1)], zres.at[pl.ds(1, ZS - 1)], o2_recv).wait()
    back = jnp.concatenate([zres[j, q] for j in range(ZS) for q in range(PLANE)], axis=0)
    back = jnp.transpose(back)
    total = jnp.zeros((128, rows), f32)
    for _ in range(3):
        part = back.astype(bf16)
        total += jnp.dot(part, onehot[...], preferred_element_type=f32)
        back = back - part.astype(f32)
    out_ref[...] = jnp.sum(jnp.where(at_lane, total, 0.0), axis=0, keepdims=True)

    def drain(ref, sem):
        pltpu.make_async_copy(ref, ref, sem).wait()

    drain(snd.at[pl.ds(1, ZS - 1)], z_send)
    drain(rsnd.at[pl.ds(1, ZS - 1)], zr_send)
    drain(prcv.at[:, pl.ds(0, PLANE - 1)], p_send)
    drain(prk.at[pl.ds(0, PLANE - 1)], pr_send)
    drain(own, s_send)
    drain(rown, sr_send)
    drain(pres.at[pl.ds(0, PLANE - 1)], o1_send)
    drain(zres.at[pl.ds(1, ZS - 1)], o2_send)


def body(embeddings, cluster_id, rank):
    rows, width = embeddings.shape
    half = width // 2
    blocks = (ZS, PLANE, 2 * CAP, half)
    small = (ZS, PLANE, 1, 128)
    vmem = pltpu.VMEM
    dma = pltpu.SemaphoreType.DMA
    out = pl.pallas_call(
        kernel,
        out_shape=jax.ShapeDtypeStruct((1, rows), f32),
        in_specs=[
            pl.BlockSpec(memory_space=pl.ANY),
            pl.BlockSpec(memory_space=vmem),
            pl.BlockSpec(memory_space=vmem),
        ],
        out_specs=pl.BlockSpec(memory_space=vmem),
        scratch_shapes=[
            vmem((rows, width), bf16),
            vmem((rows, width), bf16),
            vmem((ZS * PLANE, rows), bf16),
            vmem(blocks, bf16),
            vmem(blocks, bf16),
            vmem(blocks, bf16),
            vmem((ZS, BLOCK, width), bf16),
            vmem((ZS, BLOCK, width), bf16),
            vmem(small, f32),
            vmem(small, f32),
            vmem((PLANE, ZS, 1, 128), f32),
            vmem((ZS, 1, 128), f32),
            vmem((ZS, 1, 128), f32),
            vmem((ZS, BLOCK, BLOCK), f32),
            vmem((ZS, BLOCK, BLOCK), f32),
            vmem((ZS, 1, 128), f32),
            vmem((PLANE, ZS, 1, 128), f32),
            vmem(small, f32),
            dma, dma, dma((ZS,)), dma, dma, dma, dma((ZS,)), dma, dma,
            dma((ZS,)), dma, dma((ZS,)), dma, dma, dma, dma, dma, dma, dma,
        ],
        compiler_params=pltpu.CompilerParams(
            collective_id=0, has_side_effects=True, vmem_limit_bytes=40 << 20
        ),
        name="exchange_and_score",
    )(embeddings, cluster_id.reshape(1, rows), rank.reshape(1, rows))
    return out.reshape(rows)


def solution(mesh):
    in_specs = (P(("ingest", "span"), None), P(("ingest", "span")), P(("ingest", "span")))
    out_specs = P(("ingest", "span"))
    return jax.shard_map(body, mesh=mesh, in_specs=in_specs, out_specs=out_specs, check_vma=False)
```

time: 133 us -> 73.8 us (0.55)
  Pallas kernels: 0 us -> 70.6 us
  blocking collectives: 59.3 us -> 0 us
  waiting for transfers between devices: 21.1 us -> 0 us
  starting transfers between devices: 15.1 us -> 0 us
  between operations: 13.5 us -> 0.01 us
  matrix products: 7.64 us -> 0 us
  local copies, waits for them, and re-layouts: 9.83 us -> 3.08 us
  other arithmetic: 6.04 us -> 0 us
    pallas_call x0 -> x1, Pallas kernels: none -> 70.6 us  [body(): pl.pallas_call(kernel, out_shape=jax.ShapeDtypeStruct((1, rows), f32), in...]
    all_to_all x1 -> x0, blocking collectives: 55 us -> none  [body(): lax.all_to_all(outgoing, 'ingest', split_axis=0, concat_axis=0, tiled=True)]
    all_to_all x2 -> x0, waiting for transfers between devices: 21.1 us -> none  [the longest x1 10.6 us: body(): lax.all_to_all(highest.reshape(nodes, capacity), 'ingest', split_axis=0,...]
    all_to_all x2 -> x0, starting transfers between devices: 15.1 us -> none  [the longest x1 8.93 us: body(): lax.all_to_all(outgoing_rank, 'ingest', split_axis=0, concat_axis=0, tile...]
    dot_general x2 -> x0, matrix products: 7.64 us -> none  [tile_maxima(): jnp.einsum('qd,kd->qk', queries, candidates, preferred_element_type=jnp.f...]
    all_gather x1 -> x0, blocking collectives: 4.31 us -> none  [body(): lax.all_gather(arrived_rank, 'span', axis=0, tiled=True)]
    gather x1 -> x0, local copies, waits for them, and re-layouts: 3.42 us -> none  [body(): return returned.reshape(slots)[target]]
    scatter x1 -> x0, other arithmetic: 3.1 us -> none  [body(): outgoing = jnp.zeros((slots, width), jnp.bfloat16).at[target].set(normed)...]
  transfers between devices with their start and end apart: 3 -> 0, of which waited for: 2 -> 0; matrix products, arithmetic and copies ran while one was open for 3% -> 0% of each run, Pallas kernels for 0% -> 0%
where the time goes in v1:
time: 73.8 us; the launch traced here: 73.7 us
  Pallas kernels  70.6 us (96%)
  local copies, waits for them, and re-layouts  3.08 us (4%)
    pallas_call x1, Pallas kernels, body(): pl.pallas_call(kernel, out_shape=jax.ShapeDtypeStruct((1, rows), f32), in...  70.6 us
    unnamed x7, local copies, waits for them, and re-layouts  3.08 us

profile of v1, /device:TPU:1, one launch (start us, length us, event | category | flops | bytes accessed | tf_op | source)
XLA Modules:
  0.0 73.7 jit_solution(17215451999993076156)
XLA Ops:
  0.0 0.0 copy-start.1
  0.0 0.7 copy-done.1
  0.7 0.0 copy-start
  0.7 1.1 %copy-done = bf16[512,768]{1,0:T(8,128)(2,1)S(1)} copy-done((bf16[512,768]{1,0:T(8,128)(2,1)S(1)}, bf16[512,768]{1,0:T(8,128)(2,1)}, u32[]{:S(2)}) %copy-start) | copy-done | bytes 786456
  1.8 0.0 copy-start.2
  1.8 0.7 copy-done.2
  2.5 70.6 %exchange_and_score.1 = f32[1,512]{1,0:T(1,128)S(1)} custom-call(bf16[512,768]{1,0:T(8,128)(2,1)S(1)} %copy-done, s32[1,512]{1,0:T(1,128)S(1)} %bitcast.4, s32[1,512]{1,0:T(1,128)S(1)} %bitcast.5), custom_call_target="tpu_custom_call" | custom-call | tf_op jit(solution)/shard_map/exchange_and_score/pallas_call | solution.py:263
  73.1 0.6 copy.5
Async XLA Ops:
  0.0 0.7 copy-start.1
  0.7 1.1 %copy-start = (bf16[512,768]{1,0:T(8,128)(2,1)S(1)}, bf16[512,768]{1,0:T(8,128)(2,1)}, u32[]{:S(2)}) copy-start(bf16[512,768]{1,0:T(8,128)(2,1)} %emb_hbm.1) | copy-start | bytes 2359300
  1.8 0.7 copy-start.2

commit v2 on v1

--- a/solution.py
+++ b/solution.py
@@ -20,10 +20,10 @@
 
 
 def kernel(
-    emb_hbm, cid_ref, rank_ref, out_ref,
-    emb, normed, onehot, snd, zrcv, prcv, own, sib,
+    emb_hbm, cid_hbm, rank_hbm, out_ref,
+    emb, cid_ref, rank_ref, normed, onehot, snd, zrcv, prcv, own, sib,
     rsnd, zrk, prk, rown, rsib, qrank, acc, res, pres, zres,
-    emb_sem, z_send, z_recv, zr_send, zr_recv, p_send, p_recv, pr_send, pr_recv,
+    emb_sem, cid_sem, rank_sem, z_send, z_recv, zr_send, zr_recv, p_send, p_recv, pr_send, pr_recv,
     loc, s_send, s_recv, sr_send, sr_recv, o1_send, o1_recv, o2_send, o2_recv, loc_small,
 ):
     rows = cid_ref.shape[1]
@@ -46,8 +46,12 @@
 
     sibling = (me, 1 - core)
 
+    load_cid = pltpu.make_async_copy(cid_hbm, cid_ref, cid_sem)
+    load_cid.start()
     load = pltpu.make_async_copy(emb_hbm, emb, emb_sem)
     load.start()
+    load_rank = pltpu.make_async_copy(rank_hbm, rank_ref, rank_sem)
+    load_rank.start()
     barrier = pltpu.get_barrier_semaphore()
     for offset in range(1, ZS):
         pl.semaphore_signal(barrier, inc=1, device_id=z_peer(offset), device_id_type=MESH)
@@ -59,6 +63,7 @@
     lax.fori_loop(1, PLANE, greet, 0)
     pl.semaphore_signal(barrier, inc=1, device_id=sibling, device_id_type=MESH)
 
+    load_cid.wait()
     cid = cid_ref[...]
     cx, cz, cy = cid >> 5, (cid >> 2) & 7, cid & 3
     dz = (cz - z) & 7
@@ -75,19 +80,6 @@
     lane = mine * CAP + place
     at_lane = lax.broadcasted_iota(i32, (128, rows), 0) == lane
 
-    number = rank_ref[...] + 1
-    table = jnp.zeros((ZS * PLANE, 128), f32)
-    for shift in (0, 6, 12):
-        digit = ((number >> shift) & 63).astype(f32)
-        spread = jnp.where(at_lane, digit, 0.0).astype(bf16)
-        table += contract_last(onehot[...], spread) * float(1 << shift)
-    for t in range(ZS * PLANE):
-        row = table[t : t + 1, :]
-        if t < PLANE:
-            zrk[0, t] = row
-        else:
-            rsnd[t // PLANE, t % PLANE] = row
-
     load.wait()
     wide = emb[...].astype(f32)
     scale = lax.rsqrt(jnp.sum(wide * wide, axis=1, keepdims=True) + 1e-06)
@@ -120,15 +112,89 @@
         lax.fori_loop(1, PLANE, one, 0)
         pltpu.make_async_copy(source.at[j, mine], prcv.at[j, mine], loc.at[j]).start()
 
+    def rank_along():
+        load_rank.wait()
+        number = rank_ref[...] + 1
+        table = jnp.zeros((ZS * PLANE, 128), f32)
+        for shift in (0, 6, 12):
+            digit = ((number >> shift) & 63).astype(f32)
+            spread = jnp.where(at_lane, digit, 0.0).astype(bf16)
+            table += contract_last(onehot[...], spread) * float(1 << shift)
+        for t in range(ZS * PLANE):
+            row = table[t : t + 1, :]
+            if t < PLANE:
+                zrk[0, t] = row
+            else:
+                rsnd[t // PLANE, t % PLANE] = row
+        for j in range(1, ZS):
+            pltpu.make_async_remote_copy(
+                src_ref=rsnd.at[j], dst_ref=zrk.at[j], send_sem=zr_send, recv_sem=zr_recv,
+                device_id=z_peer(Z_OFFSETS[j]), device_id_type=MESH,
+            ).start()
+
+    def rank_within():
+        arrived = zrk.at[pl.ds(1, ZS - 1)]
+        pltpu.make_async_copy(arrived, arrived, zr_recv).wait()
+
+        def one(r, carry):
+            q, device = plane_peer(r)
+            pltpu.make_async_remote_copy(
+                src_ref=zrk.at[:, q], dst_ref=prk.at[mine], send_sem=pr_send, recv_sem=pr_recv,
+                device_id=device, device_id_type=MESH,
+            ).start()
+            return carry
+
+        lax.fori_loop(1, PLANE, one, 0)
+        pltpu.make_async_copy(zrk.at[:, mine], prk.at[mine], loc_small).start()
+
+    def rank_done():
+        pltpu.make_async_copy(prk.at[mine], prk.at[mine], loc_small).wait()
+        others = prk.at[pl.ds(0, PLANE - 1)]
+        pltpu.make_async_copy(others, others, pr_recv).wait()
+        found = jnp.sum(prk[...], axis=0)
+        rown[...] = jnp.where(found == 0.0, BEYOND, found - 1.0)
+        pltpu.make_async_remote_copy(
+            src_ref=rown, dst_ref=rsib, send_sem=sr_send, recv_sem=sr_recv,
+            device_id=sibling, device_id_type=MESH,
+        ).start()
+        for i in range(ZS):
+            qrank[i] = jnp.transpose(jnp.broadcast_to(rown[i], (BLOCK, BLOCK)))
+
+    def hand_over(j):
+        blocks = prcv.at[j, pl.ds(0, PLANE - 1)]
+        pltpu.make_async_copy(blocks, blocks, p_recv.at[j]).wait()
+        pltpu.make_async_copy(prcv.at[j, mine], prcv.at[j, mine], loc.at[j]).wait()
+        block = prcv[j].astype(f32)
+        low = block[:, :CAP, :].reshape(BLOCK, half)
+        high = block[:, CAP:, :].reshape(BLOCK, half)
+        own[j] = jnp.concatenate([low, high], axis=1).astype(bf16)
+        pltpu.make_async_remote_copy(
+            src_ref=own.at[j], dst_ref=sib.at[j], send_sem=s_send, recv_sem=s_recv.at[j],
+            device_id=sibling, device_id_type=MESH,
+        ).start()
+
+    def score(i, j):
+        keys = jnp.concatenate([own[j], sib[j]], axis=0)
+        scores = contract_last(own[i], keys)
+        theirs = qrank[i]
+        near = jnp.where(rown[j] < theirs, scores[:, :BLOCK], -1.0)
+        far = jnp.where(rsib[j] < theirs, scores[:, BLOCK:], -1.0)
+        acc[i] = jnp.maximum(acc[i], jnp.maximum(near, far))
+
+    def scores_of(j):
+        pltpu.make_async_copy(sib.at[j], sib.at[j], s_recv.at[j]).wait()
+        if j == 0:
+            pltpu.make_async_copy(rsib, rsib, sr_recv).wait()
+        for i in range(j + 1):
+            score(i, j)
+        for k in range(j):
+            score(j, k)
+
     place_rows(1, 2)
     pl.semaphore_wait(barrier, ZS - 1 + PLANE - 1 + 1)
-    for j in range(1, ZS):
-        pltpu.make_async_remote_copy(
-            src_ref=rsnd.at[j], dst_ref=zrk.at[j], send_sem=zr_send, recv_sem=zr_recv,
-            device_id=z_peer(Z_OFFSETS[j]), device_id_type=MESH,
-        ).start()
     send_z(1)
     send_z(2)
+    rank_along()
     place_rows(3, 2)
     send_z(3)
     send_z(4)
@@ -139,72 +205,23 @@
     send_z(7)
     place_rows(0, 1)
     send_plane(snd, 0)
-
-    pltpu.make_async_copy(rsnd.at[pl.ds(1, ZS - 1)], zrk.at[pl.ds(1, ZS - 1)], zr_recv).wait()
-
-    def rank_on(r, carry):
-        q, device = plane_peer(r)
-        pltpu.make_async_remote_copy(
-            src_ref=zrk.at[:, q], dst_ref=prk.at[mine], send_sem=pr_send, recv_sem=pr_recv,
-            device_id=device, device_id_type=MESH,
-        ).start()
-        return carry
-
-    lax.fori_loop(1, PLANE, rank_on, 0)
-    own_rank = pltpu.make_async_copy(zrk.at[:, mine], prk.at[mine], loc_small)
-    own_rank.start()
     acc[...] = jnp.full(acc.shape, -1.0, f32)
-    own_rank.wait()
-    pltpu.make_async_copy(prk.at[pl.ds(0, PLANE - 1)], prk.at[pl.ds(0, PLANE - 1)], pr_recv).wait()
-    found = jnp.sum(prk[...], axis=0)
-    rown[...] = jnp.where(found == 0.0, BEYOND, found - 1.0)
-    pltpu.make_async_remote_copy(
-        src_ref=rown, dst_ref=rsib, send_sem=sr_send, recv_sem=sr_recv,
-        device_id=sibling, device_id_type=MESH,
-    ).start()
-    for i in range(ZS):
-        qrank[i] = jnp.transpose(jnp.broadcast_to(rown[i], (BLOCK, BLOCK)))
-
-    def hand_over(j):
-        blocks = prcv.at[j, pl.ds(0, PLANE - 1)]
-        pltpu.make_async_copy(blocks, blocks, p_recv.at[j]).wait()
-        pltpu.make_async_copy(prcv.at[j, mine], prcv.at[j, mine], loc.at[j]).wait()
-        block = prcv[j].astype(f32)
-        low = block[:, :CAP, :].reshape(BLOCK, half)
-        high = block[:, CAP:, :].reshape(BLOCK, half)
-        own[j] = jnp.concatenate([low, high], axis=1).astype(bf16)
-        pltpu.make_async_remote_copy(
-            src_ref=own.at[j], dst_ref=sib.at[j], send_sem=s_send, recv_sem=s_recv.at[j],
-            device_id=sibling, device_id_type=MESH,
-        ).start()
-
-    def score(i, j):
-        keys = jnp.concatenate([own[j], sib[j]], axis=0)
-        scores = contract_last(own[i], keys)
-        theirs = qrank[i]
-        near = jnp.where(rown[j] < theirs, scores[:, :BLOCK], -1.0)
-        far = jnp.where(rsib[j] < theirs, scores[:, BLOCK:], -1.0)
-        acc[i] = jnp.maximum(acc[i], jnp.maximum(near, far))
-
-    def scores_of(j):
-        pltpu.make_async_copy(sib.at[j], sib.at[j], s_recv.at[j]).wait()
-        if j == 0:
-            pltpu.make_async_copy(rsib, rsib, sr_recv).wait()
-        for i in range(j + 1):
-            score(i, j)
-        for k in range(j):
-            score(j, k)
-
-    hand_over(0)
+
+    meanwhile = {
+        1: [],
+        2: [rank_within],
+        3: [lambda: hand_over(0)],
+        4: [lambda: hand_over(1), rank_done],
+        5: [lambda: hand_over(2), lambda: scores_of(0), lambda: scores_of(1)],
+        6: [lambda: hand_over(3), lambda: scores_of(2), lambda: hand_over(4), lambda: scores_of(3)],
+        7: [lambda: hand_over(5), lambda: scores_of(4), lambda: hand_over(6), lambda: scores_of(5),
+            lambda: scores_of(6), lambda: hand_over(7), lambda: scores_of(7)],
+    }
     for j in range(1, ZS):
         pltpu.make_async_copy(zrcv.at[j], zrcv.at[j], z_recv.at[j]).wait()
         send_plane(zrcv, j)
-        if j >= 2:
-            hand_over(j - 1)
-            scores_of(j - 2)
-    scores_of(ZS - 2)
-    hand_over(ZS - 1)
-    scores_of(ZS - 1)
+        for step in meanwhile[j]:
+            step()
 
     for i in range(ZS):
         res[i] = jnp.max(jnp.transpose(acc[i]), axis=0, keepdims=True)
@@ -264,13 +281,15 @@
         kernel,
         out_shape=jax.ShapeDtypeStruct((1, rows), f32),
         in_specs=[
-            pl.BlockSpec(memory_space=pl.ANY),
-            pl.BlockSpec(memory_space=vmem),
-            pl.BlockSpec(memory_space=vmem),
+            pl.BlockSpec(memory_space=pltpu.HBM),
+            pl.BlockSpec(memory_space=pltpu.HBM),
+            pl.BlockSpec(memory_space=pltpu.HBM),
         ],
         out_specs=pl.BlockSpec(memory_space=vmem),
         scratch_shapes=[
             vmem((rows, width), bf16),
+            vmem((1, rows), i32),
+            vmem((1, rows), i32),
             vmem((rows, width), bf16),
             vmem((ZS * PLANE, rows), bf16),
             vmem(blocks, bf16),
@@ -288,7 +307,7 @@
             vmem((ZS, 1, 128), f32),
             vmem((PLANE, ZS, 1, 128), f32),
             vmem(small, f32),
-            dma, dma, dma((ZS,)), dma, dma, dma, dma((ZS,)), dma, dma,
+            dma, dma, dma, dma, dma((ZS,)), dma, dma, dma, dma((ZS,)), dma, dma,
             dma((ZS,)), dma, dma((ZS,)), dma, dma, dma, dma, dma, dma, dma,
         ],
         compiler_params=pltpu.CompilerParams(

time: 73.8 us -> 73.1 us (level)
  no operation moved by 1% of the time
where the time goes in v2:
time: 73.1 us; the launch traced here: 72.9 us
  Pallas kernels  69.9 us (96%)
  local copies, waits for them, and re-layouts  3.08 us (4%)
    pallas_call x1, Pallas kernels, body(): pl.pallas_call(kernel, out_shape=jax.ShapeDtypeStruct((1, rows), f32), in...  69.9 us
    unnamed x7, local copies, waits for them, and re-layouts  3.08 us

profile of v2, /device:TPU:1, one launch (start us, length us, event | category | flops | bytes accessed | tf_op | source)
XLA Modules:
  0.0 72.9 jit_solution(18153530621501448172)
XLA Ops:
  0.0 0.0 copy-start.1
  0.0 0.7 copy-done.1
  0.7 0.0 copy-start
  0.7 1.1 %copy-done = bf16[512,768]{1,0:T(8,128)(2,1)S(1)} copy-done((bf16[512,768]{1,0:T(8,128)(2,1)S(1)}, bf16[512,768]{1,0:T(8,128)(2,1)}, u32[]{:S(2)}) %copy-start) | copy-done | bytes 786456
  1.8 0.0 copy-start.2
  1.8 0.7 copy-done.2
  2.5 69.9 %exchange_and_score.1 = f32[1,512]{1,0:T(1,128)S(1)} custom-call(bf16[512,768]{1,0:T(8,128)(2,1)S(1)} %copy-done, s32[1,512]{1,0:T(1,128)S(1)} %bitcast.4, s32[1,512]{1,0:T(1,128)S(1)} %bitcast.5), custom_call_target="tpu_custom_call" | custom-call | tf_op jit(solution)/shard_map/exchange_and_score/pallas_call | solution.py:280
  72.4 0.6 copy.5
Async XLA Ops:
  0.0 0.7 copy-start.1
  0.7 1.1 %copy-start = (bf16[512,768]{1,0:T(8,128)(2,1)S(1)}, bf16[512,768]{1,0:T(8,128)(2,1)}, u32[]{:S(2)}) copy-start(bf16[512,768]{1,0:T(8,128)(2,1)} %emb_hbm.1) | copy-start | bytes 2359300
  1.8 0.7 copy-start.2

commit v3 on v2

v3 whole, which is shorter than its diff:
```python
import jax
import jax.numpy as jnp
from jax import lax
from jax.experimental import pallas as pl
from jax.experimental.pallas import tpu as pltpu
from jax.sharding import PartitionSpec as P

XS, ZS, YS = 4, 8, 4
PLANE = XS * YS
CAP = 8
BLOCK = PLANE * CAP
BEYOND = float(2**30)
MESH = pl.DeviceIdType.MESH
Z_OFFSETS = (0, 1, 7, 2, 6, 3, 5, 4)
UNITS = tuple((j, 0, PLANE) for j in range(ZS - 1)) + ((ZS - 1, 0, PLANE // 2), (ZS - 1, PLANE // 2, PLANE))
f32, bf16, i32 = jnp.float32, jnp.bfloat16, jnp.int32


def contract_last(a, b):
    return lax.dot_general(a, b, (((1,), (1,)), ((), ())), preferred_element_type=f32)


def kernel(
    emb_hbm, cid_hbm, rank_hbm, out_ref,
    emb, cid_ref, rank_ref, normed, onehot, snd, zrcv, prcv, own, sib,
    rsnd, prk, rmid, rraw, rown, rsib, key_rank, acc, res, zres, zmid, fin,
    emb_sem, cid_sem, rank_sem, z_send, z_recv, p_send, p_recv, s_send, s_recv,
    r1_send, r1_recv, r2_send, r2_recv, r3_send, r3_recv, o1_send, o1_recv, o2_send, o2_recv,
):
    rows = cid_ref.shape[1]
    width = emb.shape[1]
    half = width // 2
    me = lax.axis_index("ingest")
    core = lax.axis_index("span")
    x, z, y = me // (ZS * YS), (me // YS) % ZS, me % YS

    def chip(px, pz, py):
        return (px * ZS + pz) * YS + py

    def z_peer(offset):
        return (chip(x, lax.rem(z + offset, ZS), y), core)

    def plane_peer(r):
        return (chip(lax.rem(x + r // YS, XS), z, lax.rem(y + r % YS, YS)), core)

    def plane_back(r):
        return (chip(lax.rem(x + XS - r // YS, XS), z, lax.rem(y + YS - r % YS, YS)), core)

    sibling = (me, 1 - core)

    def send(src, dst, send_sem, recv_sem, device):
        pltpu.make_async_remote_copy(
            src_ref=src, dst_ref=dst, send_sem=send_sem, recv_sem=recv_sem,
            device_id=device, device_id_type=MESH,
        ).start()

    def wait_for(ref, sem):
        pltpu.make_async_copy(ref, ref, sem).wait()

    load_cid = pltpu.make_async_copy(cid_hbm, cid_ref, cid_sem)
    load_cid.start()
    load = pltpu.make_async_copy(emb_hbm, emb, emb_sem)
    load.start()
    load_rank = pltpu.make_async_copy(rank_hbm, rank_ref, rank_sem)
    load_rank.start()
    barrier = pltpu.get_barrier_semaphore()
    for offset in range(1, ZS):
        pl.semaphore_signal(barrier, inc=1, device_id=z_peer(offset), device_id_type=MESH)
    for r in range(1, PLANE):
        pl.semaphore_signal(barrier, inc=1, device_id=plane_peer(r), device_id_type=MESH)
    pl.semaphore_signal(barrier, inc=1, device_id=sibling, device_id_type=MESH)

    load_cid.wait()
    cid = cid_ref[...]
    cx, cz, cy = cid >> 5, (cid >> 2) & 7, cid & 3
    dz = (cz - z) & 7
    step = jnp.where(dz <= 4, 2 * dz - 1, 2 * (ZS - dz))
    step = jnp.where(dz == 0, 0, step)
    across = ((cx - x) & 3) * YS + ((cy - y) & 3)
    hot = lax.broadcasted_iota(i32, (ZS * PLANE, rows), 0) == across * ZS + step
    hot_f = jnp.where(hot, 1.0, 0.0)
    onehot[...] = hot_f.astype(bf16)
    upper = lax.broadcasted_iota(i32, (rows, rows), 0) < lax.broadcasted_iota(i32, (rows, rows), 1)
    before = jnp.dot(onehot[...], jnp.where(upper, 1.0, 0.0).astype(bf16), preferred_element_type=f32)
    place = jnp.sum(hot_f * before, axis=0, keepdims=True).astype(i32)
    lane = across * CAP + place
    slot = step * BLOCK + lane
    at_lane = lax.broadcasted_iota(i32, (128, rows), 0) == lane

    load.wait()
    wide = emb[...].astype(f32)
    scale = lax.rsqrt(jnp.sum(wide * wide, axis=1, keepdims=True) + 1e-06)
    normed[...] = (wide * scale).astype(bf16)

    def place_rows(first, count):
        span = count * BLOCK
        ids = lax.broadcasted_iota(i32, (span, rows), 0) + first * BLOCK
        pick = jnp.where(ids == slot, 1.0, 0.0).astype(bf16)
        placed = jnp.dot(pick, normed[...], preferred_element_type=f32)
        placed = placed.reshape(count * PLANE, CAP, width)
        paired = jnp.concatenate([placed[:, :, :half], placed[:, :, half:]], axis=1)
        snd[first : first + count] = paired.astype(bf16).reshape(count, PLANE, 2 * CAP, half)

    def source(j):
        return snd if j == 0 else zrcv

    def send_z(u):
        j, lo, hi = UNITS[u]
        some = pl.ds(lo, hi - lo)
        send(snd.at[j, some], zrcv.at[j, some], z_send, z_recv.at[u], z_peer(Z_OFFSETS[j]))

    def send_plane(u):
        j, lo, hi = UNITS[u]
        for r in range(max(lo, 1), hi):
            send(source(j).at[j, r], prcv.at[j, r], p_send, p_recv.at[u], plane_peer(r))

    def rank_within():
        load_rank.wait()
        number = rank_ref[...] + 1
        table = jnp.zeros((ZS * PLANE, 128), f32)
        for shift in (0, 6, 12):
            digit = ((number >> shift) & 63).astype(f32)
            spread = jnp.where(at_lane, digit, 0.0).astype(bf16)
            table += contract_last(onehot[...], spread) * float(1 << shift)
        rsnd[...] = table.reshape(PLANE, ZS, 128)
        for r in range(1, PLANE):
            send(rsnd.at[r], prk.at[r], r1_send, r1_recv, plane_peer(r))

    def rank_along():
        wait_for(prk.at[pl.ds(1, PLANE - 1)], r1_recv)
        found = rsnd[0] + jnp.sum(prk[1:], axis=0)
        for j in range(ZS):
            rmid[j] = found[j : j + 1]
        for j in range(1, ZS):
            send(rmid.at[j], rraw.at[j], r2_send, r2_recv, z_peer(Z_OFFSETS[j]))

    def spread_ranks(ranks, base):
        for j in range(ZS):
            key_rank[base + j] = jnp.transpose(jnp.broadcast_to(ranks[j], (BLOCK, BLOCK)))

    def rank_done():
        wait_for(rraw.at[pl.ds(1, ZS - 1)], r2_recv)
        for j in range(ZS):
            found = rmid[0] if j == 0 else rraw[j]
            rown[j] = jnp.where(found == 0.0, BEYOND, found - 1.0)
        send(rown, rsib, r3_send, r3_recv, sibling)
        spread_ranks(rown, 0)

    def rank_sibling():
        wait_for(rsib, r3_recv)
        spread_ranks(rsib, ZS)

    def hand_over(u):
        j, lo, hi = UNITS[u]
        first = max(lo, 1)
        wait_for(prcv.at[j, pl.ds(first, hi - first)], p_recv.at[u])
        block = prcv[j, first:hi]
        if lo == 0:
            block = jnp.concatenate([source(j)[j, 0:1], block], axis=0)
        block = block.astype(f32)
        size = (hi - lo) * CAP
        low = block[:, :CAP, :].reshape(size, half)
        high = block[:, CAP:, :].reshape(size, half)
        own[j, lo * CAP : hi * CAP] = jnp.concatenate([low, high], axis=1).astype(bf16)
        some = pl.ds(lo * CAP, size)
        send(own.at[j, some], sib.at[j, some], s_send, s_recv.at[u], sibling)

    def score(keys, ranks, queries):
        first, count = queries
        wanted = own[first : first + count].reshape(count * BLOCK, width)
        scores = contract_last(keys, wanted)
        for i in range(count):
            part = scores[:, i * BLOCK : (i + 1) * BLOCK]
            part = jnp.where(ranks < rown[first + i], part, -1.0)
            best = jnp.max(part.reshape(-1, 8, BLOCK), axis=0)
            acc[first + i] = jnp.maximum(acc[first + i], best)

    def keys_of(j, lo, hi):
        span = slice(lo * CAP, hi * CAP)
        keys = jnp.concatenate([own[j, span], sib[j, span]], axis=0)
        ranks = jnp.concatenate([key_rank[j, span], key_rank[ZS + j, span]], axis=0)
        return keys, ranks

    def scores_of(u):
        j, lo, hi = UNITS[u]
        some = sib.at[j, pl.ds(lo * CAP, (hi - lo) * CAP)]
        wait_for(some, s_recv.at[u])
        keys, ranks = keys_of(j, lo, hi)
        last = j + 1 if hi - lo == PLANE else j
        for i in range(0, last, 2):
            score(keys, ranks, (i, min(2, last - i)))
        if hi == PLANE:
            for k in range(j + 1 if last == j else j):
                score(*keys_of(k, 0, PLANE), (j, 1))

    place_rows(1, 2)
    pl.semaphore_wait(barrier, ZS - 1 + PLANE - 1 + 1)
    send_z(1)
    send_z(2)
    rank_within()
    place_rows(3, 2)
    send_z(3)
    send_z(4)
    place_rows(5, 2)
    send_z(5)
    send_z(6)
    place_rows(7, 1)
    send_z(7)
    send_z(8)
    place_rows(0, 1)
    send_plane(0)
    acc[...] = jnp.full(acc.shape, -1.0, f32)
    rank_along()

    meanwhile = {
        1: [],
        2: [rank_done, (hand_over, 0)],
        3: [],
        4: [rank_sibling, (hand_over, 1), (hand_over, 2), (scores_of, 0)],
        5: [(scores_of, 1), (scores_of, 2)],
        6: [(hand_over, 3), (hand_over, 4), (scores_of, 3), (scores_of, 4)],
        7: [(hand_over, 5), (hand_over, 6), (scores_of, 5)],
        8: [(scores_of, 6), (hand_over, 7), (scores_of, 7), (hand_over, 8), (scores_of, 8)],
    }
    for u in range(1, len(UNITS)):
        j, lo, hi = UNITS[u]
        wait_for(zrcv.at[j, pl.ds(lo, hi - lo)], z_recv.at[u])
        send_plane(u)
        for task in meanwhile[u]:
            if isinstance(task, tuple):
                task[0](task[1])
            else:
                task()

    for j in range(ZS):
        res[j] = jnp.max(acc[j], axis=0, keepdims=True)
    for j in range(1, ZS):
        send(res.at[j], zres.at[j], o1_send, o1_recv, z_peer(ZS - Z_OFFSETS[j]))
    wait_for(zres.at[pl.ds(1, ZS - 1)], o1_recv)
    zmid[...] = jnp.concatenate([res[0]] + [zres[j] for j in range(1, ZS)], axis=0)
    for r in range(1, PLANE):
        send(zmid, fin.at[r], o2_send, o2_recv, plane_back(r))
    at_step = lax.broadcasted_iota(i32, (ZS, rows), 0) == step
    place_of = jnp.where(at_lane, 1.0, 0.0).astype(bf16)
    wait_for(fin.at[pl.ds(1, PLANE - 1)], o2_recv)
    group = lax.broadcasted_iota(i32, (ZS, 128), 1) // CAP
    back = jnp.where(group == 0, zmid[...], 0.0)
    for r in range(1, PLANE):
        back = jnp.where(group == r, fin[r], back)
    total = jnp.zeros((ZS, rows), f32)
    for _ in range(3):
        part = back.astype(bf16)
        total += jnp.dot(part, place_of, preferred_element_type=f32)
        back = back - part.astype(f32)
    out_ref[...] = jnp.sum(jnp.where(at_step, total, 0.0), axis=0, keepdims=True)

    wait_for(snd.at[pl.ds(1, ZS - 1)], z_send)
    wait_for(prcv.at[:, pl.ds(1, PLANE - 1)], p_send)
    wait_for(own, s_send)
    wait_for(prk.at[pl.ds(1, PLANE - 1)], r1_send)
    wait_for(rraw.at[pl.ds(1, ZS - 1)], r2_send)
    wait_for(rown, r3_send)
    wait_for(zres.at[pl.ds(1, ZS - 1)], o1_send)
    wait_for(fin.at[pl.ds(1, PLANE - 1)], o2_send)


def body(embeddings, cluster_id, rank):
    rows, width = embeddings.shape
    half = width // 2
    blocks = (ZS, PLANE, 2 * CAP, half)
    vmem = pltpu.VMEM
    dma = pltpu.SemaphoreType.DMA
    out = pl.pallas_call(
        kernel,
        out_shape=jax.ShapeDtypeStruct((1, rows), f32),
        in_specs=[pl.BlockSpec(memory_space=pltpu.HBM)] * 3,
        out_specs=pl.BlockSpec(memory_space=vmem),
        scratch_shapes=[
            vmem((rows, width), bf16),
            vmem((1, rows), i32),
            vmem((1, rows), i32),
            vmem((rows, width), bf16),
            vmem((ZS * PLANE, rows), bf16),
            vmem(blocks, bf16),
            vmem(blocks, bf16),
            vmem(blocks, bf16),
            vmem((ZS, BLOCK, width), bf16),
            vmem((ZS, BLOCK, width), bf16),
            vmem((PLANE, ZS, 128), f32),
            vmem((PLANE, ZS, 128), f32),
            vmem((ZS, 1, 128), f32),
            vmem((ZS, 1, 128), f32),
            vmem((ZS, 1, 128), f32),
            vmem((ZS, 1, 128), f32),
            vmem((2 * ZS, BLOCK, BLOCK), f32),
            vmem((ZS, 8, BLOCK), f32),
            vmem((ZS, 1, 128), f32),
            vmem((ZS, 1, 128), f32),
            vmem((ZS, 128), f32),
            vmem((PLANE, ZS, 128), f32),
            dma, dma, dma, dma, dma((len(UNITS),)), dma, dma((len(UNITS),)), dma, dma((len(UNITS),)),
            dma, dma, dma, dma, dma, dma, dma, dma, dma, dma,
        ],
        compiler_params=pltpu.CompilerParams(
            collective_id=0, has_side_effects=True, vmem_limit_bytes=62 << 20
        ),
        name="exchange_and_score",
    )(embeddings, cluster_id.reshape(1, rows), rank.reshape(1, rows))
    return out.reshape(rows)


def solution(mesh):
    in_specs = (P(("ingest", "span"), None), P(("ingest", "span")), P(("ingest", "span")))
    out_specs = P(("ingest", "span"))
    return jax.shard_map(body, mesh=mesh, in_specs=in_specs, out_specs=out_specs, check_vma=False)
```

time: 73.1 us -> 78 us (1.067)
  Pallas kernels: 69.9 us -> 76.6 us
  local copies, waits for them, and re-layouts: 3.08 us -> 1.26 us
    pallas_call x1, Pallas kernels: 69.9 us -> 76.6 us  [body(): pl.pallas_call(kernel, out_shape=jax.ShapeDtypeStruct((1, rows), f32), in...]
    unnamed x7 -> x1, local copies, waits for them, and re-layouts: 3.08 us -> 1.26 us
where the time goes in v3:
time: 78 us; the launch traced here: 77.9 us
  Pallas kernels  76.6 us (98%)
  local copies, waits for them, and re-layouts  1.26 us (2%)
    pallas_call x1, Pallas kernels, body(): pl.pallas_call(kernel, out_shape=jax.ShapeDtypeStruct((1, rows), f32), in...  76.6 us

profile of v3, /device:TPU:1, one launch (start us, length us, event | category | flops | bytes accessed | tf_op | source)
XLA Modules:
  0.0 77.9 jit_solution(15014493315060552984)
XLA Ops:
  0.0 76.6 %exchange_and_score.1 = f32[1,512]{1,0:T(1,128)} custom-call(bf16[512,768]{1,0:T(8,128)(2,1)} %emb_hbm.1, s32[1,512]{1,0:T(1,128)} %bitcast.4, s32[1,512]{1,0:T(1,128)} %bitcast.5), custom_call_target="tpu_custom_call" | custom-call | tf_op jit(solution)/shard_map/exchange_and_score/pallas_call | solution.py:273
  76.7 1.3 %copy.5 = f32[512]{0:T(512)} copy(f32[512]{0:T(512)} %bitcast.3) | data formatting | bytes 4096

commit v4 on v3

--- a/solution.py
+++ b/solution.py
@@ -12,6 +12,8 @@
 BEYOND = float(2**30)
 MESH = pl.DeviceIdType.MESH
 Z_OFFSETS = (0, 1, 7, 2, 6, 3, 5, 4)
+LAST = ZS - 1
+EARLY = 5
 UNITS = tuple((j, 0, PLANE) for j in range(ZS - 1)) + ((ZS - 1, 0, PLANE // 2), (ZS - 1, PLANE // 2, PLANE))
 f32, bf16, i32 = jnp.float32, jnp.bfloat16, jnp.int32
 
@@ -22,9 +24,9 @@
 
 def kernel(
     emb_hbm, cid_hbm, rank_hbm, out_ref,
-    emb, cid_ref, rank_ref, normed, onehot, snd, zrcv, prcv, own, sib,
-    rsnd, prk, rmid, rraw, rown, rsib, key_rank, acc, res, zres, zmid, fin,
-    emb_sem, cid_sem, rank_sem, z_send, z_recv, p_send, p_recv, s_send, s_recv,
+    emb, cid_ref, rank_ref, normed, onehot, snd, early, zrcv, prcv, own, sib,
+    rsnd, zrk, rmid, prk, rown, rsib, key_rank, acc, res, zres, zmid, fin,
+    emb_sem, cid_sem, rank_sem, z_send, z_recv, p_send, p_recv, e_send, e_recv, s_send, s_recv,
     r1_send, r1_recv, r2_send, r2_recv, r3_send, r3_recv, o1_send, o1_recv, o2_send, o2_recv,
 ):
     rows = cid_ref.shape[1]
@@ -77,7 +79,7 @@
     step = jnp.where(dz <= 4, 2 * dz - 1, 2 * (ZS - dz))
     step = jnp.where(dz == 0, 0, step)
     across = ((cx - x) & 3) * YS + ((cy - y) & 3)
-    hot = lax.broadcasted_iota(i32, (ZS * PLANE, rows), 0) == across * ZS + step
+    hot = lax.broadcasted_iota(i32, (ZS * PLANE, rows), 0) == step * PLANE + across
     hot_f = jnp.where(hot, 1.0, 0.0)
     onehot[...] = hot_f.astype(bf16)
     upper = lax.broadcasted_iota(i32, (rows, rows), 0) < lax.broadcasted_iota(i32, (rows, rows), 1)
@@ -107,14 +109,23 @@
     def send_z(u):
         j, lo, hi = UNITS[u]
         some = pl.ds(lo, hi - lo)
-        send(snd.at[j, some], zrcv.at[j, some], z_send, z_recv.at[u], z_peer(Z_OFFSETS[j]))
+        src = early.at[j - EARLY, some] if j >= EARLY else snd.at[j, some]
+        send(src, zrcv.at[j, some], z_send, z_recv.at[u], z_peer(Z_OFFSETS[j]))
+
+    def send_early(j):
+        early[j - EARLY, 0] = snd[j, 0]
+        for r in range(1, PLANE):
+            send(snd.at[j, r], early.at[j - EARLY, r], e_send, e_recv.at[j - EARLY], plane_peer(r))
+
+    def early_here(j):
+        wait_for(early.at[j - EARLY, pl.ds(1, PLANE - 1)], e_recv.at[j - EARLY])
 
     def send_plane(u):
         j, lo, hi = UNITS[u]
         for r in range(max(lo, 1), hi):
             send(source(j).at[j, r], prcv.at[j, r], p_send, p_recv.at[u], plane_peer(r))
 
-    def rank_within():
+    def rank_along():
         load_rank.wait()
         number = rank_ref[...] + 1
         table = jnp.zeros((ZS * PLANE, 128), f32)
@@ -122,27 +133,28 @@
             digit = ((number >> shift) & 63).astype(f32)
             spread = jnp.where(at_lane, digit, 0.0).astype(bf16)
             table += contract_last(onehot[...], spread) * float(1 << shift)
-        rsnd[...] = table.reshape(PLANE, ZS, 128)
+        rsnd[...] = table.reshape(ZS, PLANE, 128)
+        for j in range(1, ZS):
+            send(rsnd.at[j], zrk.at[j], r1_send, r1_recv, z_peer(Z_OFFSETS[j]))
+
+    def rank_within():
+        wait_for(zrk.at[pl.ds(1, ZS - 1)], r1_recv)
+        steps = [rsnd[0]] + [zrk[j] for j in range(1, ZS)]
+        for r in range(PLANE):
+            rmid[r] = jnp.concatenate([step_rank[r : r + 1] for step_rank in steps], axis=0)
         for r in range(1, PLANE):
-            send(rsnd.at[r], prk.at[r], r1_send, r1_recv, plane_peer(r))
-
-    def rank_along():
-        wait_for(prk.at[pl.ds(1, PLANE - 1)], r1_recv)
-        found = rsnd[0] + jnp.sum(prk[1:], axis=0)
-        for j in range(ZS):
-            rmid[j] = found[j : j + 1]
-        for j in range(1, ZS):
-            send(rmid.at[j], rraw.at[j], r2_send, r2_recv, z_peer(Z_OFFSETS[j]))
+            send(rmid.at[r], prk.at[r], r2_send, r2_recv, plane_peer(r))
 
     def spread_ranks(ranks, base):
         for j in range(ZS):
             key_rank[base + j] = jnp.transpose(jnp.broadcast_to(ranks[j], (BLOCK, BLOCK)))
 
     def rank_done():
-        wait_for(rraw.at[pl.ds(1, ZS - 1)], r2_recv)
+        wait_for(prk.at[pl.ds(1, PLANE - 1)], r2_recv)
+        found = rmid[0] + jnp.sum(prk[1:], axis=0)
+        found = jnp.where(found == 0.0, BEYOND, found - 1.0)
         for j in range(ZS):
-            found = rmid[0] if j == 0 else rraw[j]
-            rown[j] = jnp.where(found == 0.0, BEYOND, found - 1.0)
+            rown[j] = found[j : j + 1]
         send(rown, rsib, r3_send, r3_recv, sibling)
         spread_ranks(rown, 0)
 
@@ -152,11 +164,12 @@
 
     def hand_over(u):
         j, lo, hi = UNITS[u]
-        first = max(lo, 1)
-        wait_for(prcv.at[j, pl.ds(first, hi - first)], p_recv.at[u])
-        block = prcv[j, first:hi]
-        if lo == 0:
-            block = jnp.concatenate([source(j)[j, 0:1], block], axis=0)
+        if j >= EARLY:
+            wait_for(zrcv.at[j, pl.ds(lo, hi - lo)], z_recv.at[u])
+            block = zrcv[j, lo:hi]
+        else:
+            wait_for(prcv.at[j, pl.ds(1, PLANE - 1)], p_recv.at[j])
+            block = jnp.concatenate([source(j)[j, 0:1], prcv[j, 1:]], axis=0)
         block = block.astype(f32)
         size = (hi - lo) * CAP
         low = block[:, :CAP, :].reshape(size, half)
@@ -197,40 +210,53 @@
     pl.semaphore_wait(barrier, ZS - 1 + PLANE - 1 + 1)
     send_z(1)
     send_z(2)
-    rank_within()
+    place_rows(5, 2)
+    send_early(5)
+    send_early(6)
+    rank_along()
     place_rows(3, 2)
     send_z(3)
     send_z(4)
-    place_rows(5, 2)
-    send_z(5)
-    send_z(6)
     place_rows(7, 1)
-    send_z(7)
-    send_z(8)
+    send_early(7)
     place_rows(0, 1)
     send_plane(0)
     acc[...] = jnp.full(acc.shape, -1.0, f32)
-    rank_along()
-
-    meanwhile = {
-        1: [],
-        2: [rank_done, (hand_over, 0)],
-        3: [],
-        4: [rank_sibling, (hand_over, 1), (hand_over, 2), (scores_of, 0)],
-        5: [(scores_of, 1), (scores_of, 2)],
-        6: [(hand_over, 3), (hand_over, 4), (scores_of, 3), (scores_of, 4)],
-        7: [(hand_over, 5), (hand_over, 6), (scores_of, 5)],
-        8: [(scores_of, 6), (hand_over, 7), (scores_of, 7), (hand_over, 8), (scores_of, 8)],
-    }
-    for u in range(1, len(UNITS)):
-        j, lo, hi = UNITS[u]
-        wait_for(zrcv.at[j, pl.ds(lo, hi - lo)], z_recv.at[u])
+
+    def pass_on(u):
+        wait_for(zrcv.at[u], z_recv.at[u])
         send_plane(u)
-        for task in meanwhile[u]:
-            if isinstance(task, tuple):
-                task[0](task[1])
-            else:
-                task()
+
+    early_here(5)
+    send_z(5)
+    early_here(6)
+    send_z(6)
+    pass_on(1)
+    pass_on(2)
+    early_here(7)
+    send_z(7)
+    send_z(8)
+    rank_within()
+    for u in range(3):
+        hand_over(u)
+    rank_done()
+    pass_on(3)
+    pass_on(4)
+    rank_sibling()
+    for u in range(3):
+        scores_of(u)
+    hand_over(3)
+    hand_over(4)
+    scores_of(3)
+    scores_of(4)
+    hand_over(5)
+    hand_over(6)
+    scores_of(5)
+    scores_of(6)
+    hand_over(7)
+    hand_over(8)
+    scores_of(7)
+    scores_of(8)
 
     for j in range(ZS):
         res[j] = jnp.max(acc[j], axis=0, keepdims=True)
@@ -256,9 +282,10 @@
 
     wait_for(snd.at[pl.ds(1, ZS - 1)], z_send)
     wait_for(prcv.at[:, pl.ds(1, PLANE - 1)], p_send)
+    wait_for(early.at[:, pl.ds(1, PLANE - 1)], e_send)
     wait_for(own, s_send)
-    wait_for(prk.at[pl.ds(1, PLANE - 1)], r1_send)
-    wait_for(rraw.at[pl.ds(1, ZS - 1)], r2_send)
+    wait_for(zrk.at[pl.ds(1, ZS - 1)], r1_send)
+    wait_for(prk.at[pl.ds(1, PLANE - 1)], r2_send)
     wait_for(rown, r3_send)
     wait_for(zres.at[pl.ds(1, ZS - 1)], o1_send)
     wait_for(fin.at[pl.ds(1, PLANE - 1)], o2_send)
@@ -282,14 +309,15 @@
             vmem((rows, width), bf16),
             vmem((ZS * PLANE, rows), bf16),
             vmem(blocks, bf16),
+            vmem((ZS - EARLY,) + blocks[1:], bf16),
             vmem(blocks, bf16),
-            vmem(blocks, bf16),
+            vmem((EARLY,) + blocks[1:], bf16),
             vmem((ZS, BLOCK, width), bf16),
             vmem((ZS, BLOCK, width), bf16),
+            vmem((ZS, PLANE, 128), f32),
+            vmem((ZS, PLANE, 128), f32),
             vmem((PLANE, ZS, 128), f32),
             vmem((PLANE, ZS, 128), f32),
-            vmem((ZS, 1, 128), f32),
-            vmem((ZS, 1, 128), f32),
             vmem((ZS, 1, 128), f32),
             vmem((ZS, 1, 128), f32),
             vmem((2 * ZS, BLOCK, BLOCK), f32),
@@ -298,7 +326,7 @@
             vmem((ZS, 1, 128), f32),
             vmem((ZS, 128), f32),
             vmem((PLANE, ZS, 128), f32),
-            dma, dma, dma, dma, dma((len(UNITS),)), dma, dma((len(UNITS),)), dma, dma((len(UNITS),)),
+            dma, dma, dma, dma, dma((len(UNITS),)), dma, dma((EARLY,)), dma, dma((ZS - EARLY,)), dma, dma((len(UNITS),)),
             dma, dma, dma, dma, dma, dma, dma, dma, dma, dma,
         ],
         compiler_params=pltpu.CompilerParams(

time: 78 us -> 61.8 us (0.79)
  Pallas kernels: 76.6 us -> 60.4 us
    pallas_call x1, Pallas kernels: 76.6 us -> 60.4 us  [body(): pl.pallas_call(kernel, out_shape=jax.ShapeDtypeStruct((1, rows), f32), in...]
where the time goes in v4:
time: 61.8 us; the launch traced here: 61.7 us
  Pallas kernels  60.4 us (98%)
  local copies, waits for them, and re-layouts  1.26 us (2%)
    pallas_call x1, Pallas kernels, body(): pl.pallas_call(kernel, out_shape=jax.ShapeDtypeStruct((1, rows), f32), in...  60.4 us
    unnamed x1, local copies, waits for them, and re-layouts  1.26 us

profile of v4, /device:TPU:1, one launch (start us, length us, event | category | flops | bytes accessed | tf_op | source)
XLA Modules:
  0.0 61.7 jit_solution(7584470506618241144)
XLA Ops:
  0.0 60.4 %exchange_and_score.1 = f32[1,512]{1,0:T(1,128)} custom-call(bf16[512,768]{1,0:T(8,128)(2,1)} %emb_hbm.1, s32[1,512]{1,0:T(1,128)} %bitcast.4, s32[1,512]{1,0:T(1,128)} %bitcast.5), custom_call_target="tpu_custom_call" | custom-call | tf_op jit(solution)/shard_map/exchange_and_score/pallas_call | solution.py:300
  60.4 1.3 %copy.5 = f32[512]{0:T(512)} copy(f32[512]{0:T(512)} %bitcast.3) | data formatting | bytes 4096

commit v5 on v4

--- a/solution.py
+++ b/solution.py
@@ -15,6 +15,16 @@
 LAST = ZS - 1
 EARLY = 5
 UNITS = tuple((j, 0, PLANE) for j in range(ZS - 1)) + ((ZS - 1, 0, PLANE // 2), (ZS - 1, PLANE // 2, PLANE))
+
+
+def distance(step, r):
+    dx, dz, dy = r // YS, Z_OFFSETS[step], r % YS
+    return min(dx, XS - dx) + min(dz, ZS - dz) + min(dy, YS - dy)
+
+
+RETURNS = sorted(
+    ((j, r) for j in range(ZS) for r in range(PLANE) if (j, r) != (0, 0)), key=lambda jr: -distance(*jr)
+)
 f32, bf16, i32 = jnp.float32, jnp.bfloat16, jnp.int32
 
 
@@ -25,9 +35,9 @@
 def kernel(
     emb_hbm, cid_hbm, rank_hbm, out_ref,
     emb, cid_ref, rank_ref, normed, onehot, snd, early, zrcv, prcv, own, sib,
-    rsnd, zrk, rmid, prk, rown, rsib, key_rank, acc, res, zres, zmid, fin,
+    rsnd, zrk, rmid, prk, rown, rsib, key_rank, acc, res, fin,
     emb_sem, cid_sem, rank_sem, z_send, z_recv, p_send, p_recv, e_send, e_recv, s_send, s_recv,
-    r1_send, r1_recv, r2_send, r2_recv, r3_send, r3_recv, o1_send, o1_recv, o2_send, o2_recv,
+    r1_send, r1_recv, r2_send, r2_recv, r3_send, r3_recv, o_send, o_recv,
 ):
     rows = cid_ref.shape[1]
     width = emb.shape[1]
@@ -260,24 +270,28 @@
 
     for j in range(ZS):
         res[j] = jnp.max(acc[j], axis=0, keepdims=True)
-    for j in range(1, ZS):
-        send(res.at[j], zres.at[j], o1_send, o1_recv, z_peer(ZS - Z_OFFSETS[j]))
-    wait_for(zres.at[pl.ds(1, ZS - 1)], o1_recv)
-    zmid[...] = jnp.concatenate([res[0]] + [zres[j] for j in range(1, ZS)], axis=0)
-    for r in range(1, PLANE):
-        send(zmid, fin.at[r], o2_send, o2_recv, plane_back(r))
+    for j, r in RETURNS:
+        px, pz = lax.rem(x + XS - r // YS, XS), lax.rem(z + ZS - Z_OFFSETS[j], ZS)
+        device = (chip(px, pz, lax.rem(y + YS - r % YS, YS)), core)
+        send(res.at[j], fin.at[j * PLANE + r], o_send, o_recv, device)
+    fin[0] = res[0]
     at_step = lax.broadcasted_iota(i32, (ZS, rows), 0) == step
     place_of = jnp.where(at_lane, 1.0, 0.0).astype(bf16)
-    wait_for(fin.at[pl.ds(1, PLANE - 1)], o2_recv)
-    group = lax.broadcasted_iota(i32, (ZS, 128), 1) // CAP
-    back = jnp.where(group == 0, zmid[...], 0.0)
-    for r in range(1, PLANE):
-        back = jnp.where(group == r, fin[r], back)
-    total = jnp.zeros((ZS, rows), f32)
+    group = lax.broadcasted_iota(i32, (1, 128), 1) // CAP
+    wait_for(fin.at[pl.ds(1, ZS * PLANE - 1)], o_recv)
+    lines = []
+    for j in range(ZS):
+        line = jnp.zeros((1, 128), f32)
+        for r in range(PLANE):
+            line = jnp.where(group == r, fin[j * PLANE + r], line)
+        lines.append(line)
+    back = jnp.concatenate(lines, axis=0)
+    parts = []
     for _ in range(3):
-        part = back.astype(bf16)
-        total += jnp.dot(part, place_of, preferred_element_type=f32)
-        back = back - part.astype(f32)
+        parts.append(back.astype(bf16))
+        back = back - parts[-1].astype(f32)
+    parts = jnp.dot(jnp.concatenate(parts, axis=0), place_of, preferred_element_type=f32)
+    total = parts[:ZS] + parts[ZS : 2 * ZS] + parts[2 * ZS :]
     out_ref[...] = jnp.sum(jnp.where(at_step, total, 0.0), axis=0, keepdims=True)
 
     wait_for(snd.at[pl.ds(1, ZS - 1)], z_send)
@@ -287,8 +301,7 @@
     wait_for(zrk.at[pl.ds(1, ZS - 1)], r1_send)
     wait_for(prk.at[pl.ds(1, PLANE - 1)], r2_send)
     wait_for(rown, r3_send)
-    wait_for(zres.at[pl.ds(1, ZS - 1)], o1_send)
-    wait_for(fin.at[pl.ds(1, PLANE - 1)], o2_send)
+    wait_for(fin.at[pl.ds(1, ZS * PLANE - 1)], o_send)
 
 
 def body(embeddings, cluster_id, rank):
@@ -323,11 +336,9 @@
             vmem((2 * ZS, BLOCK, BLOCK), f32),
             vmem((ZS, 8, BLOCK), f32),
             vmem((ZS, 1, 128), f32),
-            vmem((ZS, 1, 128), f32),
-            vmem((ZS, 128), f32),
-            vmem((PLANE, ZS, 128), f32),
+            vmem((ZS * PLANE, 1, 128), f32),
             dma, dma, dma, dma, dma((len(UNITS),)), dma, dma((EARLY,)), dma, dma((ZS - EARLY,)), dma, dma((len(UNITS),)),
-            dma, dma, dma, dma, dma, dma, dma, dma, dma, dma,
+            dma, dma, dma, dma, dma, dma, dma, dma,
         ],
         compiler_params=pltpu.CompilerParams(
             collective_id=0, has_side_effects=True, vmem_limit_bytes=62 << 20

time: 61.8 us -> 60.4 us (0.977)
  Pallas kernels: 60.4 us -> 59 us
    pallas_call x1, Pallas kernels: 60.4 us -> 59 us  [body(): pl.pallas_call(kernel, out_shape=jax.ShapeDtypeStruct((1, rows), f32), in...]
where the time goes in v5:
time: 60.4 us; the launch traced here: 60.2 us
  Pallas kernels  59 us (98%)
  local copies, waits for them, and re-layouts  1.26 us (2%)
    pallas_call x1, Pallas kernels, body(): pl.pallas_call(kernel, out_shape=jax.ShapeDtypeStruct((1, rows), f32), in...  59 us
    unnamed x1, local copies, waits for them, and re-layouts  1.26 us

profile of v5, /device:TPU:1, one launch (start us, length us, event | category | flops | bytes accessed | tf_op | source)
XLA Modules:
  0.0 60.2 jit_solution(13565638039520542012)
XLA Ops:
  0.0 59.0 %exchange_and_score.1 = f32[1,512]{1,0:T(1,128)} custom-call(bf16[512,768]{1,0:T(8,128)(2,1)} %emb_hbm.1, s32[1,512]{1,0:T(1,128)} %bitcast.4, s32[1,512]{1,0:T(1,128)} %bitcast.5), custom_call_target="tpu_custom_call" | custom-call | tf_op jit(solution)/shard_map/exchange_and_score/pallas_call | solution.py:313
  59.0 1.3 %copy.5 = f32[512]{0:T(512)} copy(f32[512]{0:T(512)} %bitcast.3) | data formatting | bytes 4096

commit v6 on v5

--- a/solution.py
+++ b/solution.py
@@ -49,14 +49,18 @@
     def chip(px, pz, py):
         return (px * ZS + pz) * YS + py
 
+    xs = [lax.rem(x + d, XS) for d in range(XS)]
+    zs = [lax.rem(z + d, ZS) for d in range(ZS)]
+    ys = [lax.rem(y + d, YS) for d in range(YS)]
+
     def z_peer(offset):
-        return (chip(x, lax.rem(z + offset, ZS), y), core)
+        return (chip(x, zs[offset], y), core)
 
     def plane_peer(r):
-        return (chip(lax.rem(x + r // YS, XS), z, lax.rem(y + r % YS, YS)), core)
-
-    def plane_back(r):
-        return (chip(lax.rem(x + XS - r // YS, XS), z, lax.rem(y + YS - r % YS, YS)), core)
+        return (chip(xs[r // YS], z, ys[r % YS]), core)
+
+    def origin(j, r):
+        return (chip(xs[-(r // YS) % XS], zs[-Z_OFFSETS[j] % ZS], ys[-(r % YS) % YS]), core)
 
     sibling = (me, 1 - core)
 
@@ -98,6 +102,9 @@
     lane = across * CAP + place
     slot = step * BLOCK + lane
     at_lane = lax.broadcasted_iota(i32, (128, rows), 0) == lane
+    at_step = lax.broadcasted_iota(i32, (ZS, rows), 0) == step
+    step_hot = jnp.where(at_step, 1.0, 0.0).astype(bf16)
+    group = lax.broadcasted_iota(i32, (1, 128), 1) // CAP
 
     load.wait()
     wide = emb[...].astype(f32)
@@ -138,22 +145,21 @@
     def rank_along():
         load_rank.wait()
         number = rank_ref[...] + 1
-        table = jnp.zeros((ZS * PLANE, 128), f32)
+        table = jnp.zeros((ZS, 128), f32)
         for shift in (0, 6, 12):
             digit = ((number >> shift) & 63).astype(f32)
             spread = jnp.where(at_lane, digit, 0.0).astype(bf16)
-            table += contract_last(onehot[...], spread) * float(1 << shift)
-        rsnd[...] = table.reshape(ZS, PLANE, 128)
+            table += contract_last(step_hot, spread) * float(1 << shift)
+        for j in range(ZS):
+            rsnd[j] = table[j : j + 1]
         for j in range(1, ZS):
             send(rsnd.at[j], zrk.at[j], r1_send, r1_recv, z_peer(Z_OFFSETS[j]))
 
     def rank_within():
         wait_for(zrk.at[pl.ds(1, ZS - 1)], r1_recv)
-        steps = [rsnd[0]] + [zrk[j] for j in range(1, ZS)]
-        for r in range(PLANE):
-            rmid[r] = jnp.concatenate([step_rank[r : r + 1] for step_rank in steps], axis=0)
+        rmid[...] = jnp.concatenate([rsnd[0]] + [zrk[j] for j in range(1, ZS)], axis=0)
         for r in range(1, PLANE):
-            send(rmid.at[r], prk.at[r], r2_send, r2_recv, plane_peer(r))
+            send(rmid, prk.at[r], r2_send, r2_recv, plane_peer(r))
 
     def spread_ranks(ranks, base):
         for j in range(ZS):
@@ -161,7 +167,9 @@
 
     def rank_done():
         wait_for(prk.at[pl.ds(1, PLANE - 1)], r2_recv)
-        found = rmid[0] + jnp.sum(prk[1:], axis=0)
+        found = rmid[...]
+        for r in range(1, PLANE):
+            found = jnp.where(group == r, prk[r], found)
         found = jnp.where(found == 0.0, BEYOND, found - 1.0)
         for j in range(ZS):
             rown[j] = found[j : j + 1]
@@ -204,21 +212,25 @@
         ranks = jnp.concatenate([key_rank[j, span], key_rank[ZS + j, span]], axis=0)
         return keys, ranks
 
+    def new_keys(u, steps):
+        j, lo, hi = UNITS[u]
+        wait_for(sib.at[j, pl.ds(lo * CAP, (hi - lo) * CAP)], s_recv.at[u])
+        keys, ranks = keys_of(j, lo, hi)
+        for i in range(0, steps, 2):
+            score(keys, ranks, (i, min(2, steps - i)))
+
+    def new_queries(j):
+        for k in range(j):
+            score(*keys_of(k, 0, PLANE), (j, 1))
+
     def scores_of(u):
-        j, lo, hi = UNITS[u]
-        some = sib.at[j, pl.ds(lo * CAP, (hi - lo) * CAP)]
-        wait_for(some, s_recv.at[u])
-        keys, ranks = keys_of(j, lo, hi)
-        last = j + 1 if hi - lo == PLANE else j
-        for i in range(0, last, 2):
-            score(keys, ranks, (i, min(2, last - i)))
-        if hi == PLANE:
-            for k in range(j + 1 if last == j else j):
-                score(*keys_of(k, 0, PLANE), (j, 1))
-
-    place_rows(1, 2)
+        new_keys(u, u + 1)
+        new_queries(u)
+
+    place_rows(1, 1)
     pl.semaphore_wait(barrier, ZS - 1 + PLANE - 1 + 1)
     send_z(1)
+    place_rows(2, 1)
     send_z(2)
     place_rows(5, 2)
     send_early(5)
@@ -265,19 +277,16 @@
     scores_of(6)
     hand_over(7)
     hand_over(8)
-    scores_of(7)
-    scores_of(8)
+    new_queries(LAST)
+    new_keys(7, ZS)
+    new_keys(8, ZS)
 
     for j in range(ZS):
         res[j] = jnp.max(acc[j], axis=0, keepdims=True)
     for j, r in RETURNS:
-        px, pz = lax.rem(x + XS - r // YS, XS), lax.rem(z + ZS - Z_OFFSETS[j], ZS)
-        device = (chip(px, pz, lax.rem(y + YS - r % YS, YS)), core)
-        send(res.at[j], fin.at[j * PLANE + r], o_send, o_recv, device)
+        send(res.at[j], fin.at[j * PLANE + r], o_send, o_recv, origin(j, r))
     fin[0] = res[0]
-    at_step = lax.broadcasted_iota(i32, (ZS, rows), 0) == step
     place_of = jnp.where(at_lane, 1.0, 0.0).astype(bf16)
-    group = lax.broadcasted_iota(i32, (1, 128), 1) // CAP
     wait_for(fin.at[pl.ds(1, ZS * PLANE - 1)], o_recv)
     lines = []
     for j in range(ZS):
@@ -327,9 +336,9 @@
             vmem((EARLY,) + blocks[1:], bf16),
             vmem((ZS, BLOCK, width), bf16),
             vmem((ZS, BLOCK, width), bf16),
-            vmem((ZS, PLANE, 128), f32),
-            vmem((ZS, PLANE, 128), f32),
-            vmem((PLANE, ZS, 128), f32),
+            vmem((ZS, 1, 128), f32),
+            vmem((ZS, 1, 128), f32),
+            vmem((ZS, 128), f32),
             vmem((PLANE, ZS, 128), f32),
             vmem((ZS, 1, 128), f32),
             vmem((ZS, 1, 128), f32),

time: 60.4 us -> 58.5 us (0.969)
  Pallas kernels: 59 us -> 57.1 us
    pallas_call x1, Pallas kernels: 59 us -> 57.1 us  [body(): pl.pallas_call(kernel, out_shape=jax.ShapeDtypeStruct((1, rows), f32), in...]
where the time goes in v6:
time: 58.5 us; the launch traced here: 58.4 us
  Pallas kernels  57.1 us (98%)
  local copies, waits for them, and re-layouts  1.26 us (2%)
    pallas_call x1, Pallas kernels, body(): pl.pallas_call(kernel, out_shape=jax.ShapeDtypeStruct((1, rows), f32), in...  57.1 us
    unnamed x1, local copies, waits for them, and re-layouts  1.26 us

profile of v6, /device:TPU:1, one launch (start us, length us, event | category | flops | bytes accessed | tf_op | source)
XLA Modules:
  0.0 58.4 jit_solution(13999727894245106223)
XLA Ops:
  0.0 57.1 %exchange_and_score.1 = f32[1,512]{1,0:T(1,128)} custom-call(bf16[512,768]{1,0:T(8,128)(2,1)} %emb_hbm.1, s32[1,512]{1,0:T(1,128)} %bitcast.4, s32[1,512]{1,0:T(1,128)} %bitcast.5), custom_call_target="tpu_custom_call" | custom-call | tf_op jit(solution)/shard_map/exchange_and_score/pallas_call | solution.py:322
  57.1 1.3 %copy.5 = f32[512]{0:T(512)} copy(f32[512]{0:T(512)} %bitcast.3) | data formatting | bytes 4096

commit v7 on v6

--- a/solution.py
+++ b/solution.py
@@ -212,12 +212,14 @@
         ranks = jnp.concatenate([key_rank[j, span], key_rank[ZS + j, span]], axis=0)
         return keys, ranks
 
-    def new_keys(u, steps):
+    def new_keys(u, steps, then=None):
         j, lo, hi = UNITS[u]
         wait_for(sib.at[j, pl.ds(lo * CAP, (hi - lo) * CAP)], s_recv.at[u])
         keys, ranks = keys_of(j, lo, hi)
-        for i in range(0, steps, 2):
+        for i in reversed(range(0, steps, 2)):
             score(keys, ranks, (i, min(2, steps - i)))
+            if then is not None:
+                then(i)
 
     def new_queries(j):
         for k in range(j):
@@ -232,13 +234,13 @@
     send_z(1)
     place_rows(2, 1)
     send_z(2)
-    place_rows(5, 2)
-    send_early(5)
-    send_early(6)
     rank_along()
     place_rows(3, 2)
     send_z(3)
     send_z(4)
+    place_rows(5, 2)
+    send_early(5)
+    send_early(6)
     place_rows(7, 1)
     send_early(7)
     place_rows(0, 1)
@@ -249,12 +251,12 @@
         wait_for(zrcv.at[u], z_recv.at[u])
         send_plane(u)
 
+    pass_on(1)
+    pass_on(2)
     early_here(5)
     send_z(5)
     early_here(6)
     send_z(6)
-    pass_on(1)
-    pass_on(2)
     early_here(7)
     send_z(7)
     send_z(8)
@@ -279,12 +281,16 @@
     hand_over(8)
     new_queries(LAST)
     new_keys(7, ZS)
-    new_keys(8, ZS)
-
-    for j in range(ZS):
-        res[j] = jnp.max(acc[j], axis=0, keepdims=True)
-    for j, r in RETURNS:
-        send(res.at[j], fin.at[j * PLANE + r], o_send, o_recv, origin(j, r))
+
+    def give_back(first):
+        for j in (first, first + 1):
+            res[j] = jnp.max(acc[j], axis=0, keepdims=True)
+        for j, r in RETURNS:
+            if j in (first, first + 1):
+                send(res.at[j], fin.at[j * PLANE + r], o_send, o_recv, origin(j, r))
+
+    new_keys(8, ZS, give_back)
+
     fin[0] = res[0]
     place_of = jnp.where(at_lane, 1.0, 0.0).astype(bf16)
     wait_for(fin.at[pl.ds(1, ZS * PLANE - 1)], o_recv)

time: 58.5 us -> 58.1 us (level)
  no operation moved by 1% of the time
where the time goes in v7:
time: 58.1 us; the launch traced here: 58 us
  Pallas kernels  56.7 us (98%)
  local copies, waits for them, and re-layouts  1.26 us (2%)
    pallas_call x1, Pallas kernels, body(): pl.pallas_call(kernel, out_shape=jax.ShapeDtypeStruct((1, rows), f32), in...  56.7 us
    unnamed x1, local copies, waits for them, and re-layouts  1.26 us

profile of v7, /device:TPU:1, one launch (start us, length us, event | category | flops | bytes accessed | tf_op | source)
XLA Modules:
  0.0 58.0 jit_solution(8352615962566446)
XLA Ops:
  0.0 56.7 %exchange_and_score.1 = f32[1,512]{1,0:T(1,128)} custom-call(bf16[512,768]{1,0:T(8,128)(2,1)} %emb_hbm.1, s32[1,512]{1,0:T(1,128)} %bitcast.4, s32[1,512]{1,0:T(1,128)} %bitcast.5), custom_call_target="tpu_custom_call" | custom-call | tf_op jit(solution)/shard_map/exchange_and_score/pallas_call | solution.py:328
  56.7 1.3 %copy.5 = f32[512]{0:T(512)} copy(f32[512]{0:T(512)} %bitcast.3) | data formatting | bytes 4096

commit v8 on v7

--- a/solution.py
+++ b/solution.py
@@ -14,7 +14,7 @@
 Z_OFFSETS = (0, 1, 7, 2, 6, 3, 5, 4)
 LAST = ZS - 1
 EARLY = 5
-UNITS = tuple((j, 0, PLANE) for j in range(ZS - 1)) + ((ZS - 1, 0, PLANE // 2), (ZS - 1, PLANE // 2, PLANE))
+UNITS = tuple((j, 0, PLANE) for j in range(ZS - 1)) + ((ZS - 1, 0, 12), (ZS - 1, 12, PLANE))
 
 
 def distance(step, r):

time: 58.1 us -> 58.3 us (level)
  no operation moved by 1% of the time
where the time goes in v8:
time: 58.3 us; the launch traced here: 58.2 us
  Pallas kernels  56.9 us (98%)
  local copies, waits for them, and re-layouts  1.26 us (2%)
    pallas_call x1, Pallas kernels, body(): pl.pallas_call(kernel, out_shape=jax.ShapeDtypeStruct((1, rows), f32), in...  56.9 us
    unnamed x1, local copies, waits for them, and re-layouts  1.26 us

profile of v8, /device:TPU:1, one launch (start us, length us, event | category | flops | bytes accessed | tf_op | source)
XLA Modules:
  0.0 58.2 jit_solution(16850033302599566375)
XLA Ops:
  0.0 56.9 %exchange_and_score.1 = f32[1,512]{1,0:T(1,128)} custom-call(bf16[512,768]{1,0:T(8,128)(2,1)} %emb_hbm.1, s32[1,512]{1,0:T(1,128)} %bitcast.4, s32[1,512]{1,0:T(1,128)} %bitcast.5), custom_call_target="tpu_custom_call" | custom-call | tf_op jit(solution)/shard_map/exchange_and_score/pallas_call | solution.py:328
  56.9 1.3 %copy.5 = f32[512]{0:T(512)} copy(f32[512]{0:T(512)} %bitcast.3) | data formatting | bytes 4096

commit v9 on v8

--- a/solution.py
+++ b/solution.py
@@ -35,7 +35,7 @@
 def kernel(
     emb_hbm, cid_hbm, rank_hbm, out_ref,
     emb, cid_ref, rank_ref, normed, onehot, snd, early, zrcv, prcv, own, sib,
-    rsnd, zrk, rmid, prk, rown, rsib, key_rank, acc, res, fin,
+    rsnd, zrk, rmid, prk, rown, rsib, key_rank, acc, earlier, res, fin,
     emb_sem, cid_sem, rank_sem, z_send, z_recv, p_send, p_recv, e_send, e_recv, s_send, s_recv,
     r1_send, r1_recv, r2_send, r2_recv, r3_send, r3_recv, o_send, o_recv,
 ):
@@ -86,6 +86,9 @@
         pl.semaphore_signal(barrier, inc=1, device_id=plane_peer(r), device_id_type=MESH)
     pl.semaphore_signal(barrier, inc=1, device_id=sibling, device_id_type=MESH)
 
+    upper = lax.broadcasted_iota(i32, (rows, rows), 0) < lax.broadcasted_iota(i32, (rows, rows), 1)
+    earlier[...] = jnp.where(upper, 1.0, 0.0).astype(bf16)
+
     load_cid.wait()
     cid = cid_ref[...]
     cx, cz, cy = cid >> 5, (cid >> 2) & 7, cid & 3
@@ -96,8 +99,7 @@
     hot = lax.broadcasted_iota(i32, (ZS * PLANE, rows), 0) == step * PLANE + across
     hot_f = jnp.where(hot, 1.0, 0.0)
     onehot[...] = hot_f.astype(bf16)
-    upper = lax.broadcasted_iota(i32, (rows, rows), 0) < lax.broadcasted_iota(i32, (rows, rows), 1)
-    before = jnp.dot(onehot[...], jnp.where(upper, 1.0, 0.0).astype(bf16), preferred_element_type=f32)
+    before = jnp.dot(onehot[...], earlier[...], preferred_element_type=f32)
     place = jnp.sum(hot_f * before, axis=0, keepdims=True).astype(i32)
     lane = across * CAP + place
     slot = step * BLOCK + lane
@@ -350,6 +352,7 @@
             vmem((ZS, 1, 128), f32),
             vmem((2 * ZS, BLOCK, BLOCK), f32),
             vmem((ZS, 8, BLOCK), f32),
+            vmem((rows, rows), bf16),
             vmem((ZS, 1, 128), f32),
             vmem((ZS * PLANE, 1, 128), f32),
             dma, dma, dma, dma, dma((len(UNITS),)), dma, dma((EARLY,)), dma, dma((ZS - EARLY,)), dma, dma((len(UNITS),)),

time: 58.3 us -> 58.3 us (level)
  no operation moved by 1% of the time
where the time goes in v9:
time: 58.3 us; the launch traced here: 58.2 us
  Pallas kernels  56.9 us (98%)
  local copies, waits for them, and re-layouts  1.26 us (2%)
    pallas_call x1, Pallas kernels, body(): pl.pallas_call(kernel, out_shape=jax.ShapeDtypeStruct((1, rows), f32), in...  56.9 us
    unnamed x1, local copies, waits for them, and re-layouts  1.26 us

profile of v9, /device:TPU:1, one launch (start us, length us, event | category | flops | bytes accessed | tf_op | source)
XLA Modules:
  0.0 58.2 jit_solution(4570973114152992839)
XLA Ops:
  0.0 56.9 %exchange_and_score.1 = f32[1,512]{1,0:T(1,128)} custom-call(bf16[512,768]{1,0:T(8,128)(2,1)} %emb_hbm.1, s32[1,512]{1,0:T(1,128)} %bitcast.4, s32[1,512]{1,0:T(1,128)} %bitcast.5), custom_call_target="tpu_custom_call" | custom-call | tf_op jit(solution)/shard_map/exchange_and_score/pallas_call | solution.py:330
  56.9 1.3 %copy.5 = f32[512]{0:T(512)} copy(f32[512]{0:T(512)} %bitcast.3) | data formatting | bytes 4096
